TPU v7x, 256 devices: a whole 4x4x8 slice. The times are simulated.
256 devices in a mesh: seq: 16 (over z, y_lo), head: 16 (over y_hi, x, core).
Axes of the slice: x: 4, y: 4 (y_hi: 2, y_lo: 2; y = y_hi * 2 + y_lo), z: 8, core: 2. Of those that a mesh axis runs over, the one named last changes fastest.
Arguments:
- normed: bfloat16 [8192, 8192], P('seq', 'head'), may hold values from -6 to 6
- output_gradient: bfloat16 [8192, 8192], P('seq', 'head'), may hold values from -6 to 6
- query_weight: bfloat16 [8192, 4096], P(None, 'head'), may hold values from -0.0625 to 0.0625
- key_value_weight: bfloat16 [8192, 2, 512], P(None, None, 'head'), may hold values from -0.0625 to 0.0625
- output_weight: bfloat16 [4096, 8192], P('head'), may hold values from -0.09375 to 0.09375
- adapter_down: bfloat16 [3, 8, 8192], replicated, may hold values from -0.0625 to 0.0625
- query_up: bfloat16 [8, 4096], P(None, 'head'), may hold values from -0.5 to 0.5
- key_value_up: bfloat16 [8, 2, 512], P(None, None, 'head'), may hold values from -0.5 to 0.5
- output_down: bfloat16 [8, 4096], P(None, 'head'), may hold values from -0.09375 to 0.09375
- output_up: bfloat16 [8, 8192], P(None, 'head'), may hold values from -0.5 to 0.5
Outputs:
- normalized_gradient: bfloat16 [8192, 8192], P('seq', 'head')
- adapter_down_gradient: float32 [3, 8, 8192], replicated
- query_up_gradient: float32 [8, 4096], P(None, 'head')
- key_value_up_gradient: float32 [8, 2, 512], P(None, None, 'head')
- output_down_gradient: float32 [8, 4096], P(None, 'head')
- output_up_gradient: float32 [8, 8192], P(None, 'head')
All inputs are finite; a program needn't handle non-finite values.
Results may differ from a plain program's by a relative error of at most 0.035.
Values may be sent and summed in bfloat16 or wider, within the bound.
A program may use at most 128 MiB of HBM per device.

v0:
```python
import math

import jax
import jax.numpy as jnp
from jax import lax
from jax.sharding import PartitionSpec as P

QUERY_HEADS = 32
KEY_VALUE_HEADS = 4
HEAD_SIZE = 128
ADAPTER_RANK = 8


adapter_scale = 2.0
rope_base = 10000.0


def swapped(array, axis, distance):
    return lax.ppermute(array, axis, [(i, i ^ 1 << distance) for i in range(lax.axis_size(axis))])


def shifted_2(value, axis, steps):
    count = lax.axis_size(axis)
    pairs = [(source, (source + steps) % count) for source in range(count)]
    return lax.ppermute(value, axis, pairs)


def rope_tables(positions):
    half_dim = HEAD_SIZE // 2
    frequency = rope_base ** (-jnp.arange(half_dim, dtype=jnp.float32) * 2.0 / HEAD_SIZE)
    angles = positions.astype(jnp.float32)[:, None] * frequency[None, :]
    return (jnp.cos(angles), jnp.sin(angles))


def apply_rotation(values, cosine_rows, sine_rows):
    half_dim = HEAD_SIZE // 2
    front_half = values[..., :half_dim]
    back_half = values[..., half_dim:]
    cos_wide = cosine_rows[:, None, :]
    sin_wide = sine_rows[:, None, :]
    return jnp.concatenate(
        [
            front_half * cos_wide - back_half * sin_wide,
            back_half * cos_wide + front_half * sin_wide,
        ],
        axis=-1,
    )


def unrotate(gradient, cosine_rows, sine_rows):
    half_dim = HEAD_SIZE // 2
    front_half = gradient[..., :half_dim]
    back_half = gradient[..., half_dim:]
    cos_wide = cosine_rows[:, None, :]
    sin_wide = sine_rows[:, None, :]
    return jnp.concatenate(
        [
            front_half * cos_wide + back_half * sin_wide,
            back_half * cos_wide - front_half * sin_wide,
        ],
        axis=-1,
    )


def contract_trailing(left, right):
    return lax.dot_general(
        left, right, (((1,), (1,)), ((), ())), preferred_element_type=jnp.float32
    )


def contract_leading(left, right):
    return lax.dot_general(
        left, right, (((0,), (0,)), ((), ())), preferred_element_type=jnp.float32
    )


def body(
    normed,
    output_gradient,
    query_weight,
    key_value_weight,
    output_weight,
    adapter_down,
    query_up,
    key_value_up,
    output_down,
    output_up,
):
    single_float = jnp.float32
    brain_float = jnp.bfloat16
    count_of_rows = normed.shape[0]
    half_rows = count_of_rows // 2
    shard_width = normed.shape[1]
    complete_width = adapter_down.shape[2]
    head_count = lax.axis_size("head")
    head_index = lax.axis_index("head")
    seq_index = lax.axis_index("seq")
    local_heads = query_weight.shape[1] // HEAD_SIZE
    col_count = key_value_weight.shape[2]
    members_per_group = QUERY_HEADS // KEY_VALUE_HEADS
    kv_heads = max(1, local_heads // members_per_group)
    per_kv = local_heads // kv_heads
    kv_first = head_index * local_heads // members_per_group
    shifted = head_index * local_heads >= QUERY_HEADS // 2
    inv_root = 1.0 / math.sqrt(HEAD_SIZE)
    positions = seq_index * count_of_rows + jnp.arange(count_of_rows, dtype=jnp.int32)
    cosine_rows, sine_rows = rope_tables(positions)
    collected = lax.all_gather(normed, "head", axis=1, tiled=True)
    down_flattened = adapter_down.reshape(3 * ADAPTER_RANK, complete_width)
    lowrank_input = contract_trailing(collected, down_flattened).astype(brain_float)
    query_projected = (
        jnp.dot(collected, query_weight, preferred_element_type=single_float)
        + adapter_scale
        * jnp.dot(lowrank_input[:, :ADAPTER_RANK], query_up, preferred_element_type=single_float)
    ).astype(brain_float)
    key_value_flattened = key_value_weight.reshape(complete_width, 2 * col_count)
    key_value_lowrank = jnp.concatenate(
        [
            jnp.dot(
                lowrank_input[:, ADAPTER_RANK : 2 * ADAPTER_RANK],
                key_value_up[:, 0],
                preferred_element_type=single_float,
            ),
            jnp.dot(
                lowrank_input[:, 2 * ADAPTER_RANK :],
                key_value_up[:, 1],
                preferred_element_type=single_float,
            ),
        ],
        axis=1,
    )
    key_value_projected = (
        jnp.dot(collected, key_value_flattened, preferred_element_type=single_float)
        + adapter_scale * key_value_lowrank
    ).astype(brain_float)
    group_span = max(1, head_count // KEY_VALUE_HEADS)
    blocks = key_value_projected[:, None, :]
    for bit_index in range(group_span.bit_length() - 1):
        partner = swapped(blocks, "head", bit_index)
        low_side = head_index >> bit_index & 1 == 0
        blocks = jnp.where(
            low_side,
            jnp.concatenate([blocks, partner], axis=1),
            jnp.concatenate([partner, blocks], axis=1),
        )
    base_head = head_index // group_span * (group_span * col_count // HEAD_SIZE)
    held_heads = (
        blocks.reshape(count_of_rows, group_span, 2, col_count)
        .transpose(0, 2, 1, 3)
        .reshape(count_of_rows, 2, group_span * col_count // HEAD_SIZE, HEAD_SIZE)
    )
    q_wide = (
        lax.optimization_barrier(query_projected)
        .astype(single_float)
        .reshape(count_of_rows, local_heads, HEAD_SIZE)
    )
    query_rows = apply_rotation(q_wide, cosine_rows, sine_rows).astype(brain_float)
    chosen_keys = lax.optimization_barrier(held_heads[:, 0]).astype(single_float)
    key_matrix_rows = apply_rotation(chosen_keys, cosine_rows, sine_rows).astype(brain_float)
    pair_rows = jnp.stack([key_matrix_rows, held_heads[:, 1]], axis=1)
    next_query, next_pair = shifted_2((query_rows[:half_rows], pair_rows[:half_rows]), "seq", -1)
    queries_rolled = jnp.where(
        shifted, jnp.concatenate([query_rows[half_rows:], next_query], axis=0), query_rows
    )
    pair_rolled = jnp.where(
        shifted, jnp.concatenate([pair_rows[half_rows:], next_pair], axis=0), pair_rows
    )
    keys_shifted = pair_rolled[:, 0]
    values_shifted = pair_rolled[:, 1]
    grouped = queries_rolled.reshape(count_of_rows, kv_heads, per_kv, HEAD_SIZE)
    scores = (
        jnp.einsum("ikgd,jkd->kgij", grouped, keys_shifted, preferred_element_type=single_float)
        * inv_root
    )
    causal = jnp.arange(count_of_rows)[None, :] <= jnp.arange(count_of_rows)[:, None]
    exp_scores = jnp.where(causal, jnp.exp(scores), 0.0)
    probs_full = exp_scores / jnp.sum(exp_scores, axis=-1, keepdims=True)
    probs_low = probs_full.astype(brain_float)
    attended_rolled = (
        jnp.einsum("kgij,jkd->ikgd", probs_low, values_shifted, preferred_element_type=single_float)
        .astype(brain_float)
        .reshape(count_of_rows, local_heads * HEAD_SIZE)
    )
    carried = shifted_2(attended_rolled[half_rows:], "seq", 1)
    attention_output = jnp.where(
        shifted, jnp.concatenate([carried, attended_rolled[:half_rows]], axis=0), attended_rolled
    )
    low_part = contract_trailing(attention_output, output_down)
    grad_full = lax.all_gather(output_gradient, "head", axis=1, tiled=True)
    back_part = contract_trailing(output_gradient, output_up)
    lowrank_output, lowrank_gradient = (
        lax.psum(low_part.astype(jnp.bfloat16), "head").astype(jnp.float32),
        lax.psum(back_part.astype(jnp.bfloat16), "head").astype(jnp.float32),
    )
    lowrank_output = lowrank_output.astype(brain_float)
    lowrank_gradient = lowrank_gradient.astype(brain_float)
    attention_gradient = (
        contract_trailing(grad_full, output_weight)
        + adapter_scale
        * jnp.dot(lowrank_gradient, output_down, preferred_element_type=single_float)
    ).astype(brain_float)
    output_up_piece = adapter_scale * contract_leading(lowrank_output, output_gradient)
    next_grad = shifted_2(attention_gradient[:half_rows], "seq", -1)
    grad_rolled = jnp.where(
        shifted,
        jnp.concatenate([attention_gradient[half_rows:], next_grad], axis=0),
        attention_gradient,
    )
    output_down_piece = adapter_scale * contract_leading(lowrank_gradient, attention_output)
    grad_grouped = grad_rolled.reshape(count_of_rows, kv_heads, per_kv, HEAD_SIZE)
    grad_prob = jnp.einsum(
        "ikgd,jkd->kgij", grad_grouped, values_shifted, preferred_element_type=single_float
    )
    row_delta = jnp.sum(probs_full * grad_prob, axis=-1, keepdims=True)
    grad_score = (probs_full * (grad_prob - row_delta)).astype(brain_float)
    dquery_rolled = inv_root * jnp.einsum(
        "kgij,jkd->ikgd", grad_score, keys_shifted, preferred_element_type=single_float
    )
    dquery_rolled = dquery_rolled.reshape(count_of_rows, local_heads, HEAD_SIZE)
    key_gradient_shifted = inv_root * jnp.einsum(
        "kgij,ikgd->jkd", grad_score, grouped, preferred_element_type=single_float
    )
    value_gradient_shifted = jnp.einsum(
        "kgij,ikgd->jkd", probs_low, grad_grouped, preferred_element_type=single_float
    )
    dpair_rolled = jnp.stack([key_gradient_shifted, value_gradient_shifted], axis=1)
    prev_query, prev_pair = (
        shifted_2(dquery_rolled[half_rows:].astype(jnp.bfloat16), "seq", 1).astype(jnp.float32),
        shifted_2(dpair_rolled[half_rows:].astype(jnp.bfloat16), "seq", 1).astype(jnp.float32),
    )
    dquery = jnp.where(
        shifted, jnp.concatenate([prev_query, dquery_rolled[:half_rows]], axis=0), dquery_rolled
    )
    dpair_token = jnp.where(
        shifted, jnp.concatenate([prev_pair, dpair_rolled[:half_rows]], axis=0), dpair_rolled
    )
    query_gradient_lowrank = (
        unrotate(dquery, cosine_rows, sine_rows)
        .reshape(count_of_rows, local_heads * HEAD_SIZE)
        .astype(brain_float)
    )
    dkey_token = unrotate(dpair_token[:, 0], cosine_rows, sine_rows)
    dpair_full = jnp.stack([dkey_token, dpair_token[:, 1]], axis=1)
    blank_buffer = jnp.zeros(
        (count_of_rows, 2, group_span * col_count // HEAD_SIZE, HEAD_SIZE), single_float
    )
    blank_buffer = lax.dynamic_update_slice_in_dim(
        blank_buffer, dpair_full, kv_first - base_head, 2
    )
    blocks = blank_buffer.reshape(count_of_rows, 2, group_span, col_count).transpose(0, 2, 1, 3)
    for bit_index in reversed(range(group_span.bit_length() - 1)):
        width_half = 1 << bit_index
        lower_half = blocks[:, :width_half]
        upper_half = blocks[:, width_half:]
        upper_side = head_index >> bit_index & 1 == 1
        kept_half = jnp.where(upper_side, upper_half, lower_half)
        sent_half = jnp.where(upper_side, lower_half, upper_half).reshape(count_of_rows, -1)
        received = swapped(sent_half.astype(jnp.bfloat16), "head", bit_index).astype(
            sent_half.dtype
        )
        blocks = kept_half + received.reshape(kept_half.shape)
    dkv_own = blocks.reshape(count_of_rows, 2 * col_count)
    dkv_low = dkv_own.astype(brain_float)
    key_gradient_lowrank = dkv_low[:, :col_count]
    value_gradient_lowrank = dkv_low[:, col_count:]
    back_part_low = jnp.concatenate(
        [
            adapter_scale * contract_trailing(query_gradient_lowrank, query_up),
            adapter_scale * contract_trailing(key_gradient_lowrank, key_value_up[:, 0]),
            adapter_scale * contract_trailing(value_gradient_lowrank, key_value_up[:, 1]),
        ],
        axis=1,
    )
    backward_lowrank = (
        lax.psum(back_part_low.astype(jnp.bfloat16), "head").astype(jnp.float32).astype(brain_float)
    )
    down_part = contract_leading(backward_lowrank, collected)
    query_up_piece = adapter_scale * contract_leading(
        lowrank_input[:, :ADAPTER_RANK], query_gradient_lowrank
    )
    key_value_up_piece = adapter_scale * jnp.stack(
        [
            contract_leading(
                lowrank_input[:, ADAPTER_RANK : 2 * ADAPTER_RANK], key_gradient_lowrank
            ),
            contract_leading(lowrank_input[:, 2 * ADAPTER_RANK :], value_gradient_lowrank),
        ],
        axis=1,
    )
    partial_term = contract_trailing(query_gradient_lowrank, query_weight) + contract_trailing(
        dkv_low, key_value_flattened
    )
    summed = lax.psum_scatter(
        partial_term.astype(jnp.bfloat16), "head", scatter_dimension=1, tiled=True
    ).astype(jnp.float32)
    down_cols = lax.dynamic_slice_in_dim(down_flattened, head_index * shard_width, shard_width, 1)
    normalized_gradient = (
        summed + jnp.dot(backward_lowrank, down_cols, preferred_element_type=single_float)
    ).astype(brain_float)
    factor_totals = (
        lax.psum(down_part.astype(jnp.bfloat16), "seq").astype(jnp.float32),
        lax.psum(query_up_piece.astype(jnp.bfloat16), "seq").astype(jnp.float32),
        lax.psum(key_value_up_piece.astype(jnp.bfloat16), "seq").astype(jnp.float32),
        lax.psum(output_down_piece.astype(jnp.bfloat16), "seq").astype(jnp.float32),
        lax.psum(output_up_piece.astype(jnp.bfloat16), "seq").astype(jnp.float32),
    )
    return (
        normalized_gradient,
        factor_totals[0].reshape(3, ADAPTER_RANK, complete_width),
        factor_totals[1],
        factor_totals[2],
        factor_totals[3],
        factor_totals[4],
    )


def solution(mesh):
    return jax.shard_map(
        body,
        mesh=mesh,
        in_specs=(
            P("seq", "head"),
            P("seq", "head"),
            P(None, "head"),
            P(None, None, "head"),
            P("head", None),
            P(),
            P(None, "head"),
            P(None, None, "head"),
            P(None, "head"),
            P(None, "head"),
        ),
        out_specs=(
            P("seq", "head"),
            P(),
            P(None, "head"),
            P(None, None, "head"),
            P(None, "head"),
            P(None, "head"),
        ),
        check_vma=False,
    )
```

profile of v0, /device:TPU:48, one launch (start us, length us, event | category | flops | bytes accessed | tf_op | source)
XLA Modules:
  0.0 577.7 jit_solution(6562480584060686937)
XLA Ops:
  7.2 0.7 all-gather.3.cloned.1.call-update
  8.0 0.7 all-gather.5.cloned.1.call-update
  8.7 1.3 convolution_convert_fusion.4
  10.0 35.9 %psum.56 = bf16[512,8]{0,1:T(8,128)(2,1)S(1)} all-reduce(bf16[512,8]{0,1:T(8,128)(2,1)S(1)} %convolution_convert_fusion.4), channel_id=1, replica_groups=mesh['seq'=16,'head'=16] {'head'}, use_global_device_ids=true, to_apply=%region_1.2 | all-reduce | flops 4096 | bytes 16384 | tf_op jit(solution)/shard_map/psum | solution.py:193
  46.0 0.8 fusion.76
  46.8 0.5 multiply_cosine_fusion.1
  47.3 48.5 %all-gather.3.cloned.1.call-done = bf16[512,8192]{1,0:T(8,128)(2,1)} async-done(((bf16[512,512]{1,0:T(8,128)(2,1)}), bf16[512,8192]{1,0:T(8,128)(2,1)}) %all-gather.3.cloned.1.call-update) | async-done | bytes 8388624 | tf_op jit(solution)/shard_map/all_gather | solution.py:108
  95.9 5.8 %convolution_convert_fusion.3 = bf16[512,24]{0,1:T(8,128)(2,1)S(1)} fusion(bf16[512,8192]{1,0:T(8,128)(2,1)} %all-gather.3.cloned.1.call-done, bf16[3,8,8192]{2,1,0:T(8,128)(2,1)S(1)} %copy-done.4), kind=kOutput, calls=%fused_computation.28 | convolution fusion | flops 201338880 | bytes 8806400 | tf_op jit(solution)/shard_map/dot_general | solution.py:66
  101.6 0.2 fusion.59
  101.9 0.2 fusion.62
  102.1 2.7 fusion.13
  104.7 0.3 collective-permute-start
  105.1 77.1 %all-gather.5.cloned.1.call-done = bf16[512,8192]{1,0:T(8,128)(2,1)} async-done(((bf16[512,512]{1,0:T(8,128)(2,1)}), bf16[512,8192]{1,0:T(8,128)(2,1)}) %all-gather.5.cloned.1.call-update) | async-done | bytes 8388624 | tf_op jit(solution)/shard_map/all_gather | solution.py:189
  182.2 7.1 %fusion.78 = f32[512,256]{1,0:T(8,128)S(1)} fusion(bf16[512,8192]{1,0:T(8,128)(2,1)} %all-gather.5.cloned.1.call-done, bf16[256,8192]{1,0:T(8,128)(2,1)} %param.14), kind=kOutput, calls=%fused_computation.145 | convolution fusion | flops 2147483648 | bytes 13107200 | tf_op jit(solution)/shard_map/dot_general | solution.py:66
  189.3 0.3 fusion.9
  189.6 2.1 collective-permute-start.4
  191.7 5.8 %fusion.77 = f32[512,256]{1,0:T(8,128)S(1)} fusion(bf16[512,8192]{1,0:T(8,128)(2,1)} %all-gather.3.cloned.1.call-done, bf16[8192,256]{1,0:T(8,128)(2,1)S(1)} %copy-done.3), kind=kOutput, calls=%fused_computation.144 | convolution fusion | flops 2147483648 | bytes 13107200 | tf_op jit(solution)/shard_map/dot_general | solution.py:112
  197.5 0.3 fusion.10
  198.0 1.3 collective-permute-start.1
  199.3 0.7 fusion.45
  200.0 3.5 collective-permute-done.1
  203.9 1.2 fusion.36
  205.2 0.7 fusion.73
  205.9 1.3 collective-permute-start.2
  207.5 3.7 collective-permute-done.2
  211.2 1.0 fusion.33
  212.2 1.6 fusion.5
  213.8 0.8 convolution_convert_fusion.1
  214.6 0.6 convolution_bitcast_fusion
  215.2 0.8 fusion.1
  216.0 0.6 fusion.20
  216.6 0.3 convolution_multiply_fusion
  217.0 0.7 fusion.44
  217.6 1.4 fusion.12
  219.0 0.7 fusion.42
  219.7 1.3 collective-permute-start.6
  221.1 0.8 copy.85
  221.9 0.8 copy.86
  222.6 1.7 collective-permute-start.9
  224.4 1.3 collective-permute-start.5
  225.7 1.6 collective-permute-done.6
  227.3 0.9 convert_element_type.163
  228.3 1.2 fusion.39
  230.0 1.3 collective-permute-start.7
  231.6 1.1 convolution_convert_fusion.2
  232.7 2.4 collective-permute-done.7
  235.2 0.3 collective-permute-start.8
  235.6 1.1 collective-permute-done.8
  237.0 8.1 %fusion.79 = f32[512,8192]{1,0:T(8,128)} fusion(bf16[512,64]{0,1:T(8,128)(2,1)S(1)} %bitcast.196, bf16[8192,64]{0,1:T(8,128)(2,1)S(1)} %bitcast.180), kind=kOutput, calls=%fused_computation.146 | convolution fusion | flops 536870912 | bytes 17891328 | tf_op jit(solution)/shard_map/dot_general | solution.py:66
  245.1 68.9 %all-reduce = (bf16[512,24]{0,1:T(8,128)(2,1)S(1)}, bf16[512,8]{1,0:T(8,128)(2,1)S(1)}) all-reduce(bf16[512,24]{0,1:T(8,128)(2,1)S(1)} %pad_maximum_fusion.6, bf16[512,8]{1,0:T(8,128)(2,1)S(1)} %convolution_convert_fusion.2), channel_id=1, replica_groups=mesh['seq'=16,'head'=16] {'head'}, use_global_device_ids=true, to_apply=%region_4.5 | all-reduce | flops 16384 | bytes 65536 | tf_op jit(solution)/shard_map/psum | solution.py:275
  314.0 5.3 fusion
  319.4 12.7 %add_convert_fusion = bf16[512,8192]{1,0:T(8,128)(2,1)} fusion(f32[512,8192]{1,0:T(8,128)} %fusion.79, bf16[512,256]{0,1:T(8,128)(2,1)S(1)} %bitcast.182, bf16[8192,256]{1,0:T(8,128)(2,1)} %param.12), kind=kOutput, calls=%fused_computation | convolution fusion | flops 2155872256 | bytes 29622272 | tf_op jit(solution)/shard_map/dot_general | solution.py:66
  332.1 0.2 fusion.18
  332.3 1.1 fusion.19
  333.7 0.2 fusion.17
  333.9 64.1 %all-reduce.1 = (bf16[8,2,32]{2,0,1:T(8,128)(2,1)S(1)}, bf16[8,256]{1,0:T(8,128)(2,1)S(1)}, bf16[8,256]{1,0:T(8,128)(2,1)S(1)}, bf16[8,512]{1,0:T(8,128)(2,1)S(1)}) all-reduce(bf16[8,2,32]{2,0,1:T(8,128)(2,1)S(1)} %fusion.55, bf16[8,256]{1,0:T(8,128)(2,1)S(1)} %fusion.18, ...), channel_id=1, replica_groups=mesh['seq'=16,'head'=16] {'seq'}, use_global_device_ids=true, to_apply=%region_7.8 | all-reduce | flops 8704 | bytes 34816 | tf_op jit(solution)/shard_map/psum | solution.py:303
  398.0 0.6 copy.69
  398.6 0.6 convert_element_type.175
  399.2 0.6 convert_element_type.182
  399.8 0.6 convert_element_type.185
  400.4 54.2 %all-reduce.4.cloned.1.call-done = bf16[3,8,8192]{2,1,0:T(8,128)(2,1)} async-done(((bf16[3,8,8192]{2,1,0:T(8,128)(2,1)}), bf16[3,8,8192]{2,1,0:T(8,128)(2,1)}) %all-reduce.4.cloned.1.call-update) | async-done | bytes 393232 | tf_op jit(solution)/shard_map/psum | solution.py:301
  454.6 1.9 reshape.471
  456.5 112.5 %reduce-scatter.2.cloned.1.call-done = bf16[512,512]{1,0:T(8,128)(2,1)} async-done(((bf16[512,8192]{1,0:T(8,128)(2,1)}), bf16[512,512]{1,0:T(8,128)(2,1)}) %reduce-scatter.2.cloned.1.call-update) | async-done | bytes 524304 | tf_op jit(solution)/shard_map/reduce_scatter | solution.py:293
  569.0 2.2 fusion.6
  (71 shorter events, 3.1 us)
Async XLA Ops:
  7.2 94.9 %copy-start = (bf16[8192,2,32]{0,2,1:T(8,128)(2,1)S(1)}, bf16[8192,2,32]{0,2,1:T(8,128)(2,1)}, u32[]{:S(2)}) copy-start(bf16[8192,2,32]{0,2,1:T(8,128)(2,1)} %param.13) | copy-start | bytes 3145732
  7.2 88.7 %copy-start.4 = (bf16[3,8,8192]{2,1,0:T(8,128)(2,1)S(1)}, bf16[3,8,8192]{2,1,0:T(8,128)(2,1)}, u32[]{:S(2)}) copy-start(bf16[3,8,8192]{2,1,0:T(8,128)(2,1)} %param.15) | copy-start | bytes 1179652
  7.2 88.7 %all-gather.3.cloned.1.call-start = ((), (), s32[]{:S(2)}) async-start(), calls=%async_computation.1 | async-start | bytes 8912896 | tf_op jit(solution)/shard_map/all_gather | solution.py:108
  7.9 174.2 %all-gather.5.cloned.1.call-start = ((), (), s32[]{:S(2)}) async-start(), calls=%async_computation.2 | async-start | bytes 8912896 | tf_op jit(solution)/shard_map/all_gather | solution.py:189
  8.7 445.9 %all-reduce.4.cloned.1.call-start = ((), (), s32[]{:S(2)}) async-start(), calls=%async_computation.4 | async-start | bytes 786432 | tf_op jit(solution)/shard_map/psum | solution.py:301
  95.9 6.2 %copy-start.1 = (bf16[512,8192]{1,0:T(8,128)(2,1)S(1)}, bf16[512,8192]{1,0:T(8,128)(2,1)}, u32[]{:S(2)}) copy-start(bf16[512,8192]{1,0:T(8,128)(2,1)} %all-gather.3.cloned.1.call-done) | copy-start | bytes 25165828
  104.7 84.5 %copy-start.7 = (bf16[8,256]{1,0:T(8,128)(2,1)S(1)}, bf16[8,256]{1,0:T(8,128)(2,1)}, u32[]{:S(2)}) copy-start(bf16[8,256]{1,0:T(8,128)(2,1)} %param.18) | copy-start | bytes 12292
  104.7 93.3 %collective-permute-start = (bf16[512,1,64]{0,2,1:T(8,128)(2,1)S(1)}, bf16[512,1,64]{0,2,1:T(8,128)(2,1)S(1)}, u32[]{:S(2)}, u32[]{:S(2)}) collective-permute-start(bf16[512,1,64]{0,2,1:T(8,128)(2,1)S(1)} %bitcast.199), channel_id=1, source_target_pairs={{0,1},{1,0},{2,3},{3,2},{4,5},{5,4},{6,7},{7,6},{8,9},{9,8},{10,11... | collective-permute-start | bytes 196616 | tf_op jit(solution)/shard_map/ppermute | solution.py:19
  182.2 9.5 %copy-start.3 = (bf16[8192,256]{1,0:T(8,128)(2,1)S(1)}, bf16[8192,256]{1,0:T(8,128)(2,1)}, u32[]{:S(2)}) copy-start(bf16[8192,256]{1,0:T(8,128)(2,1)} %param.12) | copy-start | bytes 12582916
  189.6 7.9 %copy-start.6 = (bf16[8,256]{1,0:T(8,128)(2,1)S(1)}, bf16[8,256]{1,0:T(8,128)(2,1)}, u32[]{:S(2)}) copy-start(bf16[8,256]{1,0:T(8,128)(2,1)} %param.16) | copy-start | bytes 12292
  189.6 17.6 %collective-permute-start.4 = (bf16[256,256]{1,0:T(8,128)(2,1)S(1)}, bf16[256,256]{1,0:T(8,128)(2,1)S(1)}, u32[]{:S(2)}, u32[]{:S(2)}) collective-permute-start(bf16[256,256]{1,0:T(8,128)(2,1)S(1)} %get-tuple-element.43), channel_id=1, source_target_pairs={{0,240},{16,0},{32,16},{48,32},{64,48},{80,64},{96,80},{112,96},{1... | collective-permute-start | bytes 393224 | tf_op jit(solution)/shard_map/ppermute | solution.py:25
  198.0 5.5 collective-permute-start.1
  200.0 12.2 %collective-permute-start.3 = (bf16[256,2,128]{0,2,1:T(8,128)(2,1)}, bf16[256,2,128]{0,2,1:T(8,128)(2,1)}, u32[]{:S(2)}, u32[]{:S(2)}) collective-permute-start(bf16[256,2,128]{0,2,1:T(8,128)(2,1)} %get-tuple-element.37), channel_id=1, source_target_pairs={{0,240},{16,0},{32,16},{48,32},{64,48},{80,64},{96,80},{112,96},{1... | collective-permute-start | bytes 393224 | tf_op jit(solution)/shard_map/ppermute | solution.py:25
  205.9 5.3 collective-permute-start.2
  219.7 7.6 %collective-permute-start.6 = (bf16[256,2,1,128]{3,0,2,1:T(8,128)(2,1)}, bf16[256,2,1,128]{3,0,2,1:T(8,128)(2,1)}, u32[]{:S(2)}, u32[]{:S(2)}) collective-permute-start(bf16[256,2,1,128]{3,0,2,1:T(8,128)(2,1)} %fusion.42), channel_id=1, source_target_pairs={{0,16},{16,32},{32,48},{48,64},{64,80},{80,96},{96,112},{112,128},... | collective-permute-start | bytes 393224 | tf_op jit(solution)/shard_map/ppermute | solution.py:25
  222.6 8.9 %collective-permute-start.9 = (bf16[256,256]{1,0:T(8,128)(2,1)}, bf16[256,256]{1,0:T(8,128)(2,1)}, u32[]{:S(2)}, u32[]{:S(2)}) collective-permute-start(bf16[256,256]{1,0:T(8,128)(2,1)} %copy.85), channel_id=1, source_target_pairs={{0,16},{16,32},{32,48},{48,64},{64,80},{80,96},{96,112},{112,128},... | collective-permute-start | bytes 393224 | tf_op jit(solution)/shard_map/ppermute | solution.py:25
  224.4 7.0 %collective-permute-start.5 = (bf16[256,2,128]{0,2,1:T(8,128)(2,1)}, bf16[256,2,128]{0,2,1:T(8,128)(2,1)S(1)}, u32[]{:S(2)}, u32[]{:S(2)}) collective-permute-start(bf16[256,2,128]{0,2,1:T(8,128)(2,1)} %fusion.44), channel_id=1, source_target_pairs={{0,16},{16,32},{32,48},{48,64},{64,80},{80,96},{96,112},{112,128},... | collective-permute-start | bytes 393224 | tf_op jit(solution)/shard_map/ppermute | solution.py:25
  230.0 1.6 copy-start.5
  230.0 5.1 collective-permute-start.7
  235.2 1.6 collective-permute-start.8
  319.3 249.7 %reduce-scatter.2.cloned.1.call-start = ((), (), s32[]{:S(2)}) async-start(), calls=%async_computation.3 | async-start | bytes 8912896 | tf_op jit(solution)/shard_map/reduce_scatter | solution.py:293
  332.1 1.5 copy-start.2
Sparse Core Ops, SparseCore 0:
  10.6 85.2 all-gather.2
  98.4 83.7 all-gather.4
  319.5 135.1 all-reduce.3
  459.8 109.1 reduce-scatter.1
where the time goes:
time: 581 us; the launch traced here: 578 us
  waiting for transfers between devices  306 us (53%)
  blocking collectives  169 us (29%)
  matrix products  60.6 us (10%)
  between operations  14.3 us (2%)
  other arithmetic  11.7 us (2%)
  starting transfers between devices  11 us (2%)
    reduce_scatter x1, waiting for transfers between devices, body(): lax.psum_scatter(partial_term.astype(jnp.bfloat16), 'head', scatter_dimen...  112 us
    all_gather x1, waiting for transfers between devices, body(): grad_full = lax.all_gather(output_gradient, 'head', axis=1, tiled=True)  77.1 us
    psum x1, blocking collectives, body(): lax.psum(back_part_low.astype(jnp.bfloat16), 'head').astype(jnp.float32)  68.9 us
    psum x1, blocking collectives, body(): lax.psum(key_value_up_piece.astype(jnp.bfloat16), 'seq').astype(jnp.float32)  64.1 us
    psum x1, waiting for transfers between devices, body(): lax.psum(down_part.astype(jnp.bfloat16), 'seq').astype(jnp.float32)  54.2 us
    all_gather x1, waiting for transfers between devices, body(): collected = lax.all_gather(normed, 'head', axis=1, tiled=True)  48.5 us
    dot_general x9, matrix products, contract_trailing(): lax.dot_general(left, right, (((1,), (1,)), ((), ())), preferred_element_...  36.5 us
    psum x1, blocking collectives, body(): lax.psum(back_part.astype(jnp.bfloat16), 'head').astype(jnp.float32)  35.9 us
  transfers between devices with their start and end apart: 14, of which 10 were waited for; matrix products, arithmetic and copies ran while one was open for 9% of the time, Pallas kernels for 0%

commit v1 on v0

v1 whole, which is shorter than its diff:
```python
import math

import jax
import jax.numpy as jnp
from jax import lax
from jax.experimental import pallas as pl
from jax.experimental.pallas import tpu as pltpu
from jax.sharding import PartitionSpec as P

MESH = pl.DeviceIdType.MESH
F32 = jnp.float32
BF16 = jnp.bfloat16

HEAD_SIZE = 128
RANK = 8
SCALE = 2.0
ROPE_BASE = 10000.0
ROWS = 512
HALF = 256
BLK = 512
SEQ = 16
LANES = 8
TOKENS = 8192
INV_ROOT = 1.0 / math.sqrt(HEAD_SIZE)


def dot(a, b):
    return lax.dot_general(a, b, (((1,), (0,)), ((), ())), preferred_element_type=F32)


def dot_nt(a, b):
    return lax.dot_general(a, b, (((1,), (1,)), ((), ())), preferred_element_type=F32)


def dot_tn(a, b):
    return lax.dot_general(a, b, (((0,), (0,)), ((), ())), preferred_element_type=F32)


def kernel(
    x_ref, g_ref, wq_ref, wkvd_ref, wo_ref, qup_ref, kvup_ref, od_ref, up_ref, cos_ref, sin_ref,
    dx_ref, dgrad_ref, qg_ref, kvg_ref, odg_ref, oug_ref,
    buf, wqa, wqb, wkv, wkvs, woa, wob, upb, qups, kvur, kvf,
    acc_q0, acc_q1, acc_kd, acc_g0, acc_g1, acc_lg,
    sq, sqr, lip, lipr, kvp, kvr, sg, sgr, slg, slgr,
    probs, qs, ks, vs, att, gas, low, lgs, dkacc, dvacc,
    dq0, dq1, kb, lot, lotr, mown, moth, dkvr,
    st, rsr, rown, yst, yrecv, rollst, rollrecv,
    du, r1buf, pieces, r2buf, agbuf, dbuf,
    local_sem, w_send, w_recv, ag_send, ag_recv, y_send, y_recv, roll_send, roll_recv,
    m_send, m_recv, rs_send, rs_recv, s_send, s_recv,
):
    s = lax.axis_index("seq")
    h = lax.axis_index("head")
    c = lax.rem(h, 2)
    lane = h // 2
    p = lane // 4
    xi = lax.rem(lane, 4)
    a = lax.rem(xi, 2)
    q = 1 - p
    right = p * 8 + lax.rem(xi + 1, 4) * 2 + c
    left = p * 8 + lax.rem(xi + 3, 4) * 2 + c
    sib = h + 1 - 2 * c
    twin = h + 2 - 4 * a
    twin_sib = twin + 1 - 2 * c
    across = h + 8 - 16 * p

    def dev(seq, head):
        return (seq, head)

    def lane_of(r, d):
        plane = p if r == 0 else q
        return plane * 4 + lax.rem(xi + d + 4, 4)

    sends = []
    rolled_sends = []

    def remote(src, dst, ssem, rsem, device):
        return pltpu.make_async_remote_copy(
            src_ref=src, dst_ref=dst, send_sem=ssem, recv_sem=rsem,
            device_id=device, device_id_type=MESH,
        )

    def push(*ends):
        copy = remote(*ends)
        copy.start()
        sends.append(copy)

    def arrived(dst, rsem):
        pltpu.make_async_remote_copy(
            src_ref=dst, dst_ref=dst, send_sem=w_send.at[0], recv_sem=rsem,
            device_id=dev(s, sib), device_id_type=MESH,
        ).wait_recv()

    barrier = pltpu.get_barrier_semaphore()
    for d in range(1, 16):
        pl.semaphore_signal(
            barrier, inc=1, device_id=dev(s, lax.rem(h + d, 16)), device_id_type=MESH
        )
        pl.semaphore_signal(
            barrier, inc=1, device_id=dev(lax.rem(s + d, SEQ), h), device_id_type=MESH
        )
    pl.semaphore_signal(
        barrier, inc=1,
        device_id=dev(lax.rem(s + 2 * p - 1 + SEQ, SEQ), across), device_id_type=MESH,
    )

    locals_ = []

    def fetch(src, dst, k):
        copy = pltpu.make_async_copy(src, dst, local_sem.at[k])
        copy.start()
        return copy

    blocks = []
    for t, ref in enumerate((x_ref, g_ref)):
        blocks.append(fetch(ref.at[pl.ds(HALF, HALF)], buf.at[t, lane, 1 - p], t))
    for t, ref in enumerate((x_ref, g_ref)):

        @pl.when(p == 0)
        def _():
            fetch(ref.at[pl.ds(0, HALF)], buf.at[t, lane, 0], 2 + t)

    weights = [
        fetch(wq_ref.at[:, c], wqa, 4),
        fetch(wkvd_ref.at[:, c], wkv, 5),
        fetch(up_ref, upb.at[lane, pl.ds(0, 16)], 6),
    ]
    for j in range(LANES):
        cols = pl.ds(pl.multiple_of((2 * j + c) * BLK, BLK), BLK)
        weights.append(fetch(wo_ref.at[:, cols], woa.at[j], 7 + j))

    for acc in (acc_q0, acc_q1, acc_kd, acc_g0, acc_g1, acc_lg):
        acc[...] = jnp.zeros(acc.shape, F32)
    upb[:, 16:, :] = jnp.zeros((LANES, 112, BLK), BF16)
    kvf[...] = jnp.zeros(kvf.shape, BF16)

    pl.semaphore_wait(barrier, 31)

    def send_own(t, r, slot):
        b = lane_of(r, 0)
        push(buf.at[t, b, slot], buf.at[t, b, slot], ag_send.at[t, r, slot],
             ag_recv.at[t, r, slot], dev(s, right))
        push(buf.at[t, b, slot], buf.at[t, b, slot], ag_send.at[t, r, 2 + slot],
             ag_recv.at[t, r, 2 + slot], dev(s, left))

    def send_roll(t, ref):
        before = lax.rem(s + SEQ - 1, SEQ)

        def copy():
            return remote(ref.at[pl.ds(0, HALF)], buf.at[t, lane, 1], roll_send.at[t],
                          roll_recv.at[t], dev(before, h))

        rolled_sends.append(copy)

        @pl.when(p == 1)
        def _():
            copy().start()

    def send_across(t, ref):
        push(ref.at[pl.ds(0, HALF)], buf.at[t, lane, q], y_send.at[t, 0], y_recv.at[t, q],
             dev(lax.rem(s - q + SEQ, SEQ), across))
        push(ref.at[pl.ds(HALF, HALF)], buf.at[t, lane, p], y_send.at[t, 1], y_recv.at[t, p],
             dev(s, across))

    def own_ready(t):
        @pl.when(p == 0)
        def _():
            pltpu.make_async_copy(
                (x_ref, g_ref)[t].at[pl.ds(0, HALF)], buf.at[t, lane, 0], local_sem.at[2 + t]
            ).wait()

        @pl.when(p == 1)
        def _():
            arrived(buf.at[t, lane, 1], roll_recv.at[t])

    send_roll(0, x_ref)
    send_across(0, x_ref)
    send_roll(1, g_ref)
    send_across(1, g_ref)
    push(wq_ref.at[:, 1 - c], wqb, w_send.at[0], w_recv.at[0], dev(s, sib))
    push(wkvd_ref.at[:, 1 - c, :, pl.ds(0, 128)], wkvs, w_send.at[1], w_recv.at[1], dev(s, sib))
    blocks[0].wait()
    own_ready(0)
    for slot in range(2):
        send_own(0, 0, slot)
    for j in range(LANES):
        cols = pl.ds(pl.multiple_of((2 * j + 1 - c) * BLK, BLK), BLK)
        push(wo_ref.at[:, cols], wob.at[j], w_send.at[2 + j], w_recv.at[2 + j], dev(s, sib))
    blocks[1].wait()
    own_ready(1)
    for slot in range(2):
        send_own(1, 0, slot)
    weights[2].wait()
    for d in range(1, LANES):
        push(up_ref, upb.at[lane, pl.ds(0, 16)], w_send.at[10 + d], w_recv.at[10 + d],
             dev(s, lax.rem(lane + d, LANES) * 2 + c))
    push(qup_ref.at[pl.ds(0, 16)], qups, w_send.at[18], w_recv.at[18], dev(s, sib))
    for k, peer in enumerate((sib, twin, twin_sib)):
        push(kvup_ref.at[pl.ds(0, 32)], kvur.at[k], w_send.at[19 + k], w_recv.at[19 + k],
             dev(s, peer))

    def multiply(t, b):
        def rows(i, carry):
            block = buf[t, b, i]
            if t == 0:
                acc_q0[i] += dot(block, wqa[b])
                acc_q1[i] += dot(block, wqb[b])
                acc_kd[i] += dot(block, wkv[b])
            else:
                acc_g0[i] += dot_nt(block, woa[b])
                acc_g1[i] += dot_nt(block, wob[b])
                acc_lg[i] += dot_nt(block, upb[b])
            return carry

        lax.fori_loop(0, 2, rows, 0)

    def multiply_sides(t, r):
        def one(k, carry):
            multiply(t, lane_of(r, 1 + 2 * k))
            return carry

        lax.fori_loop(0, 2, one, 0)

    def forward(t, r):
        from_left, from_right = lane_of(r, -1), lane_of(r, 1)
        arrived(buf.at[t, from_left, 0], ag_recv.at[t, r, 0])
        push(buf.at[t, from_left, 0], buf.at[t, from_left, 0], ag_send.at[t, r, 4],
             ag_recv.at[t, r, 4], dev(s, right))
        arrived(buf.at[t, from_right, 1], ag_recv.at[t, r, 3])
        push(buf.at[t, from_right, 1], buf.at[t, from_right, 1], ag_send.at[t, r, 5],
             ag_recv.at[t, r, 5], dev(s, left))

    def sides_ready(t, r):
        arrived(buf.at[t, lane_of(r, -1), 1], ag_recv.at[t, r, 1])
        arrived(buf.at[t, lane_of(r, 1), 0], ag_recv.at[t, r, 2])

    def far_ready(t, r):
        far = lane_of(r, 2)
        arrived(buf.at[t, far, 0], ag_recv.at[t, r, 4])
        arrived(buf.at[t, far, 1], ag_recv.at[t, r, 5])

    def across_ready(t):
        b = lane_of(1, 0)
        for slot in range(2):
            arrived(buf.at[t, b, slot], y_recv.at[t, slot])
            send_own(t, 1, slot)

    forward(0, 0)
    across_ready(0)
    forward(1, 0)
    for k in (0, 1):
        weights[k].wait()
    arrived(wqb, w_recv.at[0])
    arrived(wkvs, w_recv.at[1])

    def join(j, carry):
        wkv[j, :, 0:128] += wkvs[j]
        return carry

    lax.fori_loop(0, LANES, join, 0)
    sides_ready(0, 0)
    across_ready(1)
    multiply(0, lane_of(0, 0))
    multiply_sides(0, 0)
    sides_ready(1, 0)
    for copy in weights[3:]:
        copy.wait()
    for j in range(LANES):
        arrived(wob.at[j], w_recv.at[2 + j])
    for d in range(1, LANES):
        arrived(upb.at[lax.rem(lane - d + LANES, LANES), pl.ds(0, 16)], w_recv.at[10 + d])
    multiply(1, lane_of(0, 0))
    multiply_sides(1, 0)
    forward(0, 1)
    far_ready(0, 0)
    multiply(0, lane_of(0, 2))
    forward(1, 1)
    multiply(0, lane_of(1, 0))
    sides_ready(0, 1)
    multiply_sides(0, 1)
    far_ready(1, 0)
    multiply(1, lane_of(0, 2))
    multiply(1, lane_of(1, 0))
    far_ready(0, 1)
    multiply(0, lane_of(1, 2))

    sq[...] = acc_q1[...].astype(BF16)
    kvp[...] = acc_kd[:, :, 0:128].astype(BF16)
    lip[...] = acc_kd[:, :, 128:256].astype(BF16)
    push(kvp, kvr.at[0], m_send.at[0], m_recv.at[0], dev(s, sib))
    push(kvp, kvr.at[1], m_send.at[1], m_recv.at[1], dev(s, twin))
    push(kvp, kvr.at[2], m_send.at[2], m_recv.at[2], dev(s, twin_sib))
    push(lip, lipr, m_send.at[3], m_recv.at[3], dev(s, sib))
    push(sq, sqr, m_send.at[4], m_recv.at[4], dev(s, sib))

    sides_ready(1, 1)
    multiply_sides(1, 1)
    far_ready(1, 1)
    multiply(1, lane_of(1, 2))
    sg[...] = acc_g1[...].astype(BF16)
    slg[...] = acc_lg[...].astype(BF16)
    push(slg, slgr, m_send.at[5], m_recv.at[5], dev(s, sib))
    push(sg, sgr, m_send.at[6], m_recv.at[6], dev(s, sib))

    for k in range(3):
        arrived(kvur.at[k], w_recv.at[19 + k])
    arrived(qups, w_recv.at[18])
    kvf[0:32, :] = kvup_ref[0:32, :] + kvur[0] + kvur[1] + kvur[2]
    arrived(kvr.at[0], m_recv.at[0])
    arrived(kvr.at[1], m_recv.at[1])
    arrived(kvr.at[2], m_recv.at[2])
    arrived(lipr, m_recv.at[3])
    arrived(sqr, m_recv.at[4])

    def rotate(v, i):
        return v * cos_ref[i] + pltpu.roll(v, 64, 1) * sin_ref[i]

    def unrotate(v, i):
        return v * cos_ref[i] - pltpu.roll(v, 64, 1) * sin_ref[i]

    def project(i, carry):
        low_i = (acc_kd[i, :, 128:256] + lipr[i].astype(F32)).astype(BF16)
        low[i] = low_i
        q_i = (acc_q0[i] + sqr[i].astype(F32) + SCALE * dot(low_i, qup_ref[...])).astype(BF16)
        for hd in range(2):
            cols = slice(hd * 128, hd * 128 + 128)
            qs[hd, i] = rotate(q_i[:, cols].astype(F32), i).astype(BF16)
        own = acc_kd[i, :, 0:128] + kvr[0, i].astype(F32)
        other = kvr[1, i].astype(F32) + kvr[2, i].astype(F32)
        first = jnp.where(a == 0, own, other)
        second = jnp.where(a == 0, other, own)
        rank = SCALE * dot(low_i, kvf[...])
        k_i = jnp.concatenate([first[:, 0:64], second[:, 0:64]], axis=1) + rank[:, 0:128]
        v_i = jnp.concatenate([first[:, 64:128], second[:, 64:128]], axis=1) + rank[:, 128:256]
        start = pl.multiple_of(i * HALF, HALF)
        ks[pl.ds(start, HALF), :] = rotate(k_i.astype(BF16).astype(F32), i).astype(BF16)
        vs[pl.ds(start, HALF), :] = v_i.astype(BF16)
        return carry

    lax.fori_loop(0, 2, project, 0)

    for i in range(2):
        keys = (i + 1) * HALF

        def attend(hd, carry):
            scores = dot_nt(qs[hd, i], ks[0:keys, :]) * INV_ROOT
            row = lax.broadcasted_iota(jnp.int32, scores.shape, 0) + i * HALF
            col = lax.broadcasted_iota(jnp.int32, scores.shape, 1)
            e = jnp.where(col <= row, jnp.exp(scores), 0.0)
            full = e / jnp.sum(e, axis=-1, keepdims=True)
            probs[hd, i, :, 0:keys] = full
            att[hd, i] = dot(full.astype(BF16), vs[0:keys, :]).astype(BF16)
            return carry

        lax.fori_loop(0, 2, attend, 0)
    loti = jnp.concatenate(
        [
            dot_nt(od_ref[0:16, 0:128], att[0, i]) + dot_nt(od_ref[0:16, 128:256], att[1, i])
            for i in range(2)
        ],
        axis=1,
    )
    lot[...] = loti.astype(BF16)
    push(lot, lotr, m_send.at[7], m_recv.at[7], dev(s, sib))

    arrived(slgr, m_recv.at[5])
    arrived(sgr, m_recv.at[6])

    def cotangent(i, carry):
        lg = (acc_lg[i] + slgr[i].astype(F32)).astype(BF16)
        lgs[i] = lg
        ga = (acc_g0[i] + sgr[i].astype(F32) + SCALE * dot(lg, od_ref[...])).astype(BF16)
        gas[0, i] = ga[:, 0:128]
        gas[1, i] = ga[:, 128:256]
        return carry

    lax.fori_loop(0, 2, cotangent, 0)
    dkacc[...] = jnp.zeros(dkacc.shape, F32)
    dvacc[...] = jnp.zeros(dvacc.shape, F32)
    for i in range(2):
        keys = (i + 1) * HALF
        for hd in range(2):
            full = probs[hd, i, :, 0:keys]
            grad = dot_nt(gas[hd, i], vs[0:keys, :])
            delta = jnp.sum(full * grad, axis=-1, keepdims=True)
            ds = (full * (grad - delta)).astype(BF16)
            dq = INV_ROOT * dot(ds, ks[0:keys, :])
            dq0[i, :, hd * 128 : hd * 128 + 128] = unrotate(dq, i).astype(BF16)
            dkacc[0:keys, :] += dot_tn(ds, qs[hd, i])
            dvacc[0:keys, :] += dot_tn(full.astype(BF16), gas[hd, i])
    push(dq0, dq1, m_send.at[8], m_recv.at[8], dev(s, sib))
    for i in range(2):
        rows = slice(i * HALF, i * HALF + HALF)
        dk = unrotate(INV_ROOT * dkacc[rows, :], i)
        dv = dvacc[rows, :]
        low_side = jnp.concatenate([dk[:, 0:64], dv[:, 0:64]], axis=1)
        high_side = jnp.concatenate([dk[:, 64:128], dv[:, 64:128]], axis=1)
        mown[i] = jnp.where(a == 0, low_side, high_side).astype(BF16)
        moth[i] = jnp.where(a == 0, high_side, low_side).astype(BF16)
    push(moth, dkvr.at[1], m_send.at[9], m_recv.at[9], dev(s, twin))
    push(moth, dkvr.at[2], m_send.at[10], m_recv.at[10], dev(s, twin_sib))
    push(mown, dkvr.at[0], m_send.at[11], m_recv.at[11], dev(s, sib))

    kv_rows = kvf[0:32, :].astype(F32)
    kv_low = jnp.concatenate([kv_rows[:, 0:64], kv_rows[:, 128:192]], axis=1)
    kv_high = jnp.concatenate([kv_rows[:, 64:128], kv_rows[:, 192:256]], axis=1)
    kv_chip = jnp.where(a == 0, kv_low, kv_high).astype(BF16)
    kv_chip = jnp.concatenate([kv_chip, jnp.zeros((96, 128), BF16)], axis=0)
    sib_up = jnp.concatenate([qups[...], jnp.zeros((112, 256), BF16)], axis=0)

    arrived(dq1, m_recv.at[8])
    arrived(dkvr.at[1], m_recv.at[9])
    arrived(dkvr.at[2], m_recv.at[10])
    arrived(dkvr.at[0], m_recv.at[11])
    back_t = []
    for i in range(2):
        total = (
            mown[i].astype(F32) + dkvr[0, i].astype(F32)
            + dkvr[1, i].astype(F32) + dkvr[2, i].astype(F32)
        ).astype(BF16)
        back = SCALE * (
            dot_nt(dq0[i], qup_ref[...]) + dot_nt(dq1[i], sib_up) + dot_nt(total, kv_chip)
        )
        kb[i, :, 0:128] = total
        kb[i, :, 128:256] = back.astype(BF16)
        back_t.append(back.T[0:32, :])

    def dx_block(b, i):
        return dot_nt(dq0[i], wqa[b]) + dot_nt(dq1[i], wqb[b]) + dot_nt(kb[i], wkv[b])

    def far_block(r):
        def one(i, carry):
            st[r, 0, i] = dx_block(lane_of(r, 2), i).astype(BF16)
            return carry

        lax.fori_loop(0, 2, one, 0)
        push(st.at[r, 0, 0], rsr.at[r, 0], rs_send.at[r, 0], rs_recv.at[r, 0], dev(s, right))
        push(st.at[r, 0, 1], rsr.at[r, 1], rs_send.at[r, 1], rs_recv.at[r, 1], dev(s, left))

    def side_free(r):
        st[r, 1, 1] = dx_block(lane_of(r, 1), 1).astype(BF16)
        push(st.at[r, 1, 1], rsr.at[r, 3], rs_send.at[r, 3], rs_recv.at[r, 3], dev(s, right))
        st[r, 2, 0] = dx_block(lane_of(r, -1), 0).astype(BF16)
        push(st.at[r, 2, 0], rsr.at[r, 4], rs_send.at[r, 4], rs_recv.at[r, 4], dev(s, left))

    def side_sum(r):
        arrived(rsr.at[r, 0], rs_recv.at[r, 0])
        st[r, 1, 0] = (dx_block(lane_of(r, 1), 0) + rsr[r, 0].astype(F32)).astype(BF16)
        push(st.at[r, 1, 0], rsr.at[r, 2], rs_send.at[r, 2], rs_recv.at[r, 2], dev(s, right))
        arrived(rsr.at[r, 1], rs_recv.at[r, 1])
        st[r, 2, 1] = (dx_block(lane_of(r, -1), 1) + rsr[r, 1].astype(F32)).astype(BF16)
        push(st.at[r, 2, 1], rsr.at[r, 5], rs_send.at[r, 5], rs_recv.at[r, 5], dev(s, left))

    def own_block(r, i):
        arrived(rsr.at[r, 2 + i], rs_recv.at[r, 2 + i])
        arrived(rsr.at[r, 4 + i], rs_recv.at[r, 4 + i])
        return dx_block(lane_of(r, 0), i) + rsr[r, 2 + i].astype(F32) + rsr[r, 4 + i].astype(F32)

    far_block(1)
    side_free(1)
    far_block(0)
    side_free(0)

    arrived(lotr, m_recv.at[7])
    back_full = jnp.concatenate(back_t, axis=1).astype(BF16)
    low_out = (SCALE * (loti + lotr[...].astype(F32))).astype(BF16)
    out_full = jnp.concatenate(
        [jnp.zeros((16, ROWS), BF16), jnp.zeros((8, ROWS), BF16), low_out[0:8]], axis=0
    )

    def adapters(j, carry):
        total = jnp.zeros((32, BLK), F32)
        for i in range(2):
            cols = slice(i * HALF, i * HALF + HALF)
            total += dot(back_full[:, cols], buf[0, j, i]) + dot(out_full[:, cols], buf[1, j, i])
        du[j] = total.astype(BF16)
        return carry

    lax.fori_loop(0, LANES, adapters, 0)
    side_sum(1)
    for d in range(1, LANES):
        owner = lax.rem(lane + d, LANES)
        push(du.at[owner], r1buf.at[d - 1], s_send.at[0, d], s_recv.at[0, d],
             dev(s, owner * 2 + c))

    low_t = jnp.concatenate([low[i].astype(F32).T[0:32] for i in range(2)], axis=1).astype(BF16)
    lg_t = jnp.concatenate([lgs[i].astype(F32).T[0:16] for i in range(2)], axis=1).astype(BF16)
    query_up = jnp.zeros((32, 256), F32)
    kv_up = jnp.zeros((32, 128), F32)
    out_down = jnp.zeros((16, 256), F32)
    for i in range(2):
        cols = slice(i * HALF, i * HALF + HALF)
        query_up += dot(low_t[:, cols], dq0[i])
        kv_up += dot(low_t[:, cols], kb[i, :, 0:128])
        out_down += jnp.concatenate(
            [dot(lg_t[:, cols], att[0, i]), dot(lg_t[:, cols], att[1, i])], axis=1
        )
    side_sum(0)
    lane_col = lax.broadcasted_iota(jnp.int32, (8, 128), 1)
    kv_grad = SCALE * jnp.where(lane_col < 64, kv_up[8:16], kv_up[16:24])
    alone = jnp.concatenate(
        [
            jnp.concatenate([SCALE * query_up[0:8], SCALE * out_down[0:8]], axis=1),
            jnp.concatenate([kv_grad, jnp.zeros((8, 384), F32)], axis=1),
        ],
        axis=0,
    ).astype(BF16)
    for k in range(4):
        pieces[8 + k] = alone[:, k * 128 : k * 128 + 128]
        pieces[12 + k] = jnp.zeros((16, 128), BF16)
    shared = du[lane].astype(F32)
    for d in range(1, LANES):
        arrived(r1buf.at[d - 1], s_recv.at[0, d])
        shared += r1buf[d - 1].astype(F32)
    shared = shared.astype(BF16)
    for g in range(2):
        for k in range(4):
            pieces[4 * g + k] = shared[16 * g : 16 * g + 16, k * 128 : k * 128 + 128]
    for d in range(1, SEQ):
        owner = lax.rem(s + d, SEQ)
        push(pieces.at[owner], r2buf.at[d - 1], s_send.at[1, d], s_recv.at[1, d], dev(owner, h))

    for i in range(2):
        yst[i] = own_block(1, i).astype(BF16)
        half = i + p - 2 * i * p
        push(yst.at[i], yrecv.at[half], y_send.at[2, i], y_recv.at[2, half],
             dev(lax.rem(s + i * p, SEQ), across))

    mine = pieces[s].astype(F32)
    for d in range(1, SEQ):
        arrived(r2buf.at[d - 1], s_recv.at[1, d])
        mine += r2buf[d - 1].astype(F32)
    agbuf[s] = mine.astype(BF16)
    for d in range(1, SEQ):
        push(agbuf.at[s], agbuf.at[s], s_send.at[2, d], s_recv.at[2, d],
             dev(lax.rem(s + d, SEQ), h))

    after = lax.rem(s + 1, SEQ)

    def send_back():
        return remote(rollst, rollrecv, roll_send.at[2], roll_recv.at[2], dev(after, h))

    rolled_sends.append(send_back)
    for i in (1, 0):
        rown[i] = own_block(0, i)
        if i == 1:

            @pl.when(p == 1)
            def _():
                rollst[...] = rown[1].astype(BF16)
                send_back().start()

    for d in range(1, SEQ):
        arrived(agbuf.at[lax.rem(s - d + SEQ, SEQ)], s_recv.at[2, d])
    for d in range(1, 16):
        push(agbuf.at[pl.ds(0, 8)], dbuf.at[h], s_send.at[3, d], s_recv.at[3, d],
             dev(s, lax.rem(h + d, 16)))
    for k in range(4):
        cols = slice(k * 128, k * 128 + 128)
        oug_ref[:, cols] = agbuf[4 + k].astype(F32)[8:16]
    for k in range(2):
        cols = slice(k * 128, k * 128 + 128)
        qg_ref[:, cols] = agbuf[8 + k].astype(F32)[0:8]
        odg_ref[:, cols] = agbuf[10 + k].astype(F32)[0:8]
    kvg_ref[...] = agbuf[8].astype(F32)[8:16]
    dbuf[h] = agbuf[0:8]

    for half in range(2):
        arrived(yrecv.at[half], y_recv.at[2, half])

    @pl.when(p == 0)
    def _():
        for i in range(2):
            dx_ref[i * HALF : i * HALF + HALF, :] = (rown[i] + yrecv[i].astype(F32)).astype(BF16)

    @pl.when(p == 1)
    def _():
        arrived(rollrecv, roll_recv.at[2])
        dx_ref[HALF:ROWS, :] = (rown[0] + yrecv[1].astype(F32)).astype(BF16)
        dx_ref[0:HALF, :] = (rollrecv[...].astype(F32) + yrecv[0].astype(F32)).astype(BF16)

    for d in range(1, 16):
        arrived(dbuf.at[lax.rem(h - d + 16, 16)], s_recv.at[3, d])

    def place(j, carry):
        for k in range(4):
            cols = pl.ds(pl.multiple_of(j * BLK + k * 128, 128), 128)
            dgrad_ref[0:16, cols] = dbuf[j, k].astype(F32)
            dgrad_ref[16:24, cols] = dbuf[j, 4 + k].astype(F32)[0:8]
        return carry

    lax.fori_loop(0, 16, place, 0)

    for copy in sends:
        copy.wait_send()

    @pl.when(p == 1)
    def _():
        for copy in rolled_sends:
            copy().wait_send()


def body(normed, output_gradient, query_weight, key_value_weight, output_weight,
         adapter_down, query_up, key_value_up, output_down, output_up):
    h = lax.axis_index("head")
    s = lax.axis_index("seq")
    c = lax.rem(h, 2)
    p = h // 8
    width = adapter_down.shape[2]

    positions = lax.rem(
        s * ROWS + jnp.arange(ROWS, dtype=jnp.int32) + p * HALF, TOKENS
    ).astype(F32)
    half_dim = HEAD_SIZE // 2
    frequency = ROPE_BASE ** (-jnp.arange(half_dim, dtype=F32) * 2.0 / HEAD_SIZE)
    angles = positions[:, None] * frequency[None, :]
    cos, sin = jnp.cos(angles), jnp.sin(angles)
    cos_wide = jnp.concatenate([cos, cos], axis=1).reshape(2, HALF, HEAD_SIZE)
    sin_wide = jnp.concatenate([-sin, sin], axis=1).reshape(2, HALF, HEAD_SIZE)

    keys, values = key_value_weight[:, 0], key_value_weight[:, 1]
    blank = jnp.zeros_like(keys)
    placed = jnp.where(
        c == 0,
        jnp.concatenate([keys, blank, values, blank], axis=1),
        jnp.concatenate([blank, keys, blank, values], axis=1),
    )
    down_t = adapter_down.reshape(3 * RANK, width).T
    wkvd = jnp.concatenate(
        [placed, down_t, jnp.zeros((width, 128 - 3 * RANK), BF16)], axis=1
    ).reshape(LANES, 2, BLK, 256)
    wq = query_weight.reshape(LANES, 2, BLK, 256)

    def tall(array, rows):
        return jnp.pad(array, ((0, rows - array.shape[0]), (0, 0)))

    column = lax.rem(h, 4) * 32
    kvup = jnp.zeros((128, 256), BF16)
    kvup = lax.dynamic_update_slice(kvup, key_value_up[:, 0], (8, column))
    kvup = lax.dynamic_update_slice(kvup, key_value_up[:, 1], (16, 128 + column))

    vm = lambda *shape: pltpu.VMEM(shape, BF16)
    vf = lambda *shape: pltpu.VMEM(shape, F32)
    dma = lambda *shape: pltpu.SemaphoreType.DMA(shape)
    out_shape = [
        jax.ShapeDtypeStruct((ROWS, BLK), BF16),
        jax.ShapeDtypeStruct((3 * RANK, width), F32),
        jax.ShapeDtypeStruct((RANK, 256), F32),
        jax.ShapeDtypeStruct((RANK, 128), F32),
        jax.ShapeDtypeStruct((RANK, 256), F32),
        jax.ShapeDtypeStruct((RANK, BLK), F32),
    ]
    hbm = pl.BlockSpec(memory_space=pl.ANY)
    vmem = pl.BlockSpec(memory_space=pltpu.VMEM)
    scratch = [
        vm(2, LANES, 2, HALF, BLK), vm(LANES, BLK, 256), vm(LANES, BLK, 256),
        vm(LANES, BLK, 256), vm(LANES, BLK, 128), vm(LANES, 256, BLK), vm(LANES, 256, BLK),
        vm(LANES, 128, BLK), vm(16, 256), vm(3, 32, 256), vm(128, 256),
        vf(2, HALF, 256), vf(2, HALF, 256), vf(2, HALF, 256), vf(2, HALF, 256),
        vf(2, HALF, 256), vf(2, HALF, 128),
        vm(2, HALF, 256), vm(2, HALF, 256), vm(2, HALF, 128), vm(2, HALF, 128),
        vm(2, HALF, 128), vm(3, 2, HALF, 128), vm(2, HALF, 256), vm(2, HALF, 256),
        vm(2, HALF, 128), vm(2, HALF, 128),
        vf(2, 2, HALF, ROWS), vm(2, 2, HALF, 128), vm(ROWS, 128), vm(ROWS, 128),
        vm(2, 2, HALF, 128), vm(2, 2, HALF, 128), vm(2, HALF, 128), vm(2, HALF, 128),
        vf(ROWS, 128), vf(ROWS, 128),
        vm(2, HALF, 256), vm(2, HALF, 256), vm(2, HALF, 256), vm(16, ROWS), vm(16, ROWS),
        vm(2, HALF, 128), vm(2, HALF, 128), vm(3, 2, HALF, 128),
        vm(2, 3, 2, HALF, BLK), vm(2, 6, HALF, BLK), vf(2, HALF, BLK), vm(2, HALF, BLK),
        vm(2, HALF, BLK), vm(HALF, BLK), vm(HALF, BLK),
        vm(LANES, 32, BLK), vm(LANES - 1, 32, BLK), vm(16, 16, 128), vm(15, 16, 128),
        vm(16, 16, 128), vm(16, 8, 16, 128),
        dma(16), dma(22), dma(22), dma(2, 2, 6), dma(2, 2, 6), dma(3, 2), dma(3, 2),
        dma(3), dma(3), dma(12), dma(12), dma(2, 6), dma(2, 6), dma(4, 16), dma(4, 16),
    ]
    dx, dgrad, qg, kvg, odg, oug = pl.pallas_call(
        kernel,
        out_shape=out_shape,
        in_specs=[hbm] * 5 + [vmem] * 3 + [hbm] + [vmem] * 2,
        out_specs=[vmem] * 6,
        scratch_shapes=scratch,
        compiler_params=pltpu.CompilerParams(
            collective_id=0, has_side_effects=True, vmem_limit_bytes=56 * 1024 * 1024
        ),
        cost_estimate=pl.CostEstimate(
            flops=9_000_000_000, bytes_accessed=20_000_000, transcendentals=400_000
        ),
    )(
        normed, output_gradient, wq, wkvd, output_weight, tall(query_up, 128), kvup,
        tall(output_down, 128), tall(output_up, 16), cos_wide, sin_wide,
    )
    kv_grad = jnp.stack(
        [
            lax.dynamic_slice_in_dim(kvg, c * 32, 32, 1),
            lax.dynamic_slice_in_dim(kvg, 64 + c * 32, 32, 1),
        ],
        axis=1,
    )
    return dx, dgrad.reshape(3, RANK, width), qg, kv_grad, odg, oug


def solution(mesh):
    return jax.shard_map(
        body,
        mesh=mesh,
        in_specs=(
            P("seq", "head"), P("seq", "head"), P(None, "head"), P(None, None, "head"),
            P("head", None), P(), P(None, "head"), P(None, None, "head"),
            P(None, "head"), P(None, "head"),
        ),
        out_specs=(
            P("seq", "head"), P(), P(None, "head"), P(None, None, "head"),
            P(None, "head"), P(None, "head"),
        ),
        check_vma=False,
    )
```

time: 581 us -> 202 us (0.35)
  the two profiles are of different devices: /device:TPU:48 before, /device:TPU:9 now
where the time goes in v1:
time: 202 us; the launch traced here: 201 us
  Pallas kernels  175 us (87%)
  local copies, waits for them, and re-layouts  19.6 us (10%)
  other arithmetic  5.97 us (3%)
    pallas_call x1, Pallas kernels, body(): pl.pallas_call(kernel, out_shape=out_shape, in_specs=[hbm] * 5 + [vmem] *...  175 us
    unnamed x17, local copies, waits for them, and re-layouts  7.86 us
    concatenate x2, local copies, waits for them, and re-layouts, body(): jnp.concatenate([placed, down_t, jnp.zeros((width, 128 - 3 * RANK), BF16)...  6.51 us

profile of v1, /device:TPU:9, one launch (start us, length us, event | category | flops | bytes accessed | tf_op | source)
XLA Modules:
  0.0 201.3 jit_solution(4957309754068352892)
XLA Ops:
  0.6 0.0 copy-start
  0.6 1.3 slice_bitcast_fusion.1
  2.0 0.5 maximum_select_fusion
  2.6 0.1 pad.22.clone
  2.7 0.0 copy-done
  2.7 2.8 %maximum_maximum_fusion = bf16[8192,256]{0,1:T(8,128)(2,1)} fusion(bf16[8192,24]{0,1:T(8,128)(2,1)S(1)} %bitcast.18, bf16[8192,128]{0,1:T(8,128)(2,1)S(1)} %maximum_select_fusion, bf16[256]{0:T(256)(128)(2,1)S(1)} %pad.22.clone), kind=kLoop, calls=%fused_computation | loop fusion | flops 12582912 | bytes 6685184 | tf_op jit(solution)/shard_map/concatenate | solution.py:629
  5.5 0.0 copy-start.4
  5.5 0.0 copy-start.2
  5.5 0.0 copy-start.5
  5.5 0.0 copy-start.3
  5.5 6.4 %copy.16 = bf16[8192,256]{1,0:T(8,128)(2,1)} copy(bf16[8192,256]{0,1:T(8,128)(2,1)} %maximum_maximum_fusion) | data formatting | bytes 8388608 | tf_op jit(solution)/shard_map/concatenate | solution.py:629
  11.9 0.0 copy-done.4
  11.9 0.6 pad.11.qup_ref
  12.5 0.0 copy-done.2
  12.6 0.6 dynamic_update_slice.6
  13.2 0.5 dynamic_update_slice.7.kvup_ref
  13.7 0.0 copy-done.5
  13.7 0.0 copy-start.1
  13.7 0.7 pad.12.od_ref
  14.4 0.0 copy-done.3
  14.4 0.6 pad.13.up_ref
  15.0 1.0 fusion
  16.0 1.0 pad_maximum_fusion
  17.0 0.0 copy-done.1
  17.0 175.0 %shard_map.145 = (bf16[512,512]{1,0:T(8,128)(2,1)}, f32[24,8192]{1,0:T(8,128)}, f32[8,256]{1,0:T(8,128)}, f32[8,128]{1,0:T(8,128)}, f32[8,256]{1,0:T(8,128)}, /*index=5*/f32[8,512]{1,0:T(8,128)}) custom-call(bf16[512,512]{1,0:T(8,128)(2,1)} %x_ref.1, bf16[512,512]{1,0:T(8,128)(2,1)} %g_ref.1, bf16[8,2,512,256]{3,2,1,0:T(8,128)(2,1)} %bitcast.21, ...), custom_call_target="tpu_custom_call" | custom-call | flops 8999999488 | bytes 20000000 | tf_op jit(solution)/shard_map/pallas_call | solution.py:676
  192.0 0.8 constant_dynamic-slice_fusion.1
  192.8 0.6 pad_maximum_fusion.2
  193.4 1.9 copy.30
  195.3 2.1 %copy.31 = f32[3,8,8192]{2,1,0:T(8,128)} copy(f32[3,8,8192]{2,1,0:T(8,128)} %bitcast.17) | data formatting | bytes 1572864
  197.4 1.3 copy.32
  198.7 1.3 copy.33
  200.0 1.3 copy.34
  (7 shorter events, 0.1 us)
Async XLA Ops:
  0.6 2.0 %copy-start = (bf16[3,8,8192]{2,1,0:T(8,128)(2,1)S(1)}, bf16[3,8,8192]{2,1,0:T(8,128)(2,1)}, u32[]{:S(2)}) copy-start(bf16[3,8,8192]{2,1,0:T(8,128)(2,1)} %param.15) | copy-start | bytes 1179652
  5.5 6.4 %copy-start.4 = (bf16[8,256]{1,0:T(8,128)(2,1)S(1)}, bf16[8,256]{1,0:T(8,128)(2,1)}, u32[]{:S(2)}) copy-start(bf16[8,256]{1,0:T(8,128)(2,1)} %param.16) | copy-start | bytes 12292
  5.5 7.1 %copy-start.2 = (bf16[8,2,32]{2,1,0:T(2,128)(2,1)S(1)}, bf16[8,2,32]{2,1,0:T(2,128)(2,1)}, u32[]{:S(2)}) copy-start(bf16[8,2,32]{2,1,0:T(2,128)(2,1)} %param.17) | copy-start | bytes 3076
  5.5 8.2 %copy-start.5 = (bf16[8,256]{1,0:T(8,128)(2,1)S(1)}, bf16[8,256]{1,0:T(8,128)(2,1)}, u32[]{:S(2)}) copy-start(bf16[8,256]{1,0:T(8,128)(2,1)} %param.18) | copy-start | bytes 12292
  5.5 8.9 %copy-start.3 = (bf16[8,512]{1,0:T(8,128)(2,1)S(1)}, bf16[8,512]{1,0:T(8,128)(2,1)}, u32[]{:S(2)}) copy-start(bf16[8,512]{1,0:T(8,128)(2,1)} %param.19) | copy-start | bytes 24580
  13.7 3.3 %copy-start.1 = (bf16[128,256]{1,0:T(8,128)(2,1)}, bf16[128,256]{1,0:T(8,128)(2,1)S(1)}, u32[]{:S(2)}) copy-start(bf16[128,256]{1,0:T(8,128)(2,1)S(1)} %dynamic_update_slice.7.kvup_ref) | copy-start | bytes 196612

commit v2 on v1

--- a/solution.py
+++ b/solution.py
@@ -37,9 +37,9 @@
 
 
 def kernel(
-    x_ref, g_ref, wq_ref, wkvd_ref, wo_ref, qup_ref, kvup_ref, od_ref, up_ref, cos_ref, sin_ref,
-    dx_ref, dgrad_ref, qg_ref, kvg_ref, odg_ref, oug_ref,
-    buf, wqa, wqb, wkv, wkvs, woa, wob, upb, qups, kvur, kvf,
+    x_ref, g_ref, wq_ref, kvt_ref, wo_ref, down_ref, qup_in, kvup_in, od_in, up_in, cos_ref, sin_ref,
+    dx_ref, dgrad_ref, small_ref,
+    buf, wqa, wqb, wkv, woa, wob, upb, qups, kvur, kvf, qup_ref, kvup_ref, od_ref, up_ref,
     acc_q0, acc_q1, acc_kd, acc_g0, acc_g1, acc_lg,
     sq, sqr, lip, lipr, kvp, kvr, sg, sgr, slg, slgr,
     probs, qs, ks, vs, att, gas, low, lgs, dkacc, dvacc,
@@ -122,26 +122,50 @@
 
     weights = [
         fetch(wq_ref.at[:, c], wqa, 4),
-        fetch(wkvd_ref.at[:, c], wkv, 5),
-        fetch(up_ref, upb.at[lane, pl.ds(0, 16)], 6),
     ]
     for j in range(LANES):
         cols = pl.ds(pl.multiple_of((2 * j + c) * BLK, BLK), BLK)
-        weights.append(fetch(wo_ref.at[:, cols], woa.at[j], 7 + j))
+        weights.append(fetch(kvt_ref.at[:, :, cols], wkv.at[j, pl.ds(0, 2), c], 5 + j))
+    for j in range(LANES):
+        cols = pl.ds(pl.multiple_of((2 * j + c) * BLK, BLK), BLK)
+        weights.append(fetch(wo_ref.at[:, cols], woa.at[j], 13 + j))
 
     for acc in (acc_q0, acc_q1, acc_kd, acc_g0, acc_g1, acc_lg):
         acc[...] = jnp.zeros(acc.shape, F32)
     upb[:, 16:, :] = jnp.zeros((LANES, 112, BLK), BF16)
     kvf[...] = jnp.zeros(kvf.shape, BF16)
+    qup_ref[...] = jnp.concatenate([qup_in[...], jnp.zeros((120, 256), BF16)], axis=0)
+    od_ref[...] = jnp.concatenate([od_in[...], jnp.zeros((120, 256), BF16)], axis=0)
+    up_ref[...] = jnp.concatenate([up_in[...], jnp.zeros((8, BLK), BF16)], axis=0)
+    upb[lane, 0:16, :] = up_ref[...]
+    source = lax.broadcasted_iota(jnp.int32, (64, 256), 0)
+    target = lax.broadcasted_iota(jnp.int32, (64, 256), 1)
+    goal = source + lax.rem(h, 4) * 32 + jnp.where(source < 32, 0, 96)
+    spread = dot(kvup_in[...], jnp.where(target == goal, 1.0, 0.0).astype(BF16))
+    column = lax.broadcasted_iota(jnp.int32, (8, 256), 1)
+    none = jnp.zeros((8, 256), F32)
+    kvup_ref[...] = jnp.concatenate(
+        [none, jnp.where(column < 128, spread, 0.0), jnp.where(column < 128, 0.0, spread), none],
+        axis=0,
+    ).astype(BF16)
+    wkv[:, 2:4] = jnp.zeros((LANES, 2, 2, 32, BLK), BF16)
+    for j in range(LANES):
+        cols = pl.ds(pl.multiple_of((2 * j + c) * BLK, BLK), BLK)
+        wkv[j, 2, 0] = jnp.concatenate([down_ref[:, cols], jnp.zeros((8, BLK), BF16)], axis=0)
 
     pl.semaphore_wait(barrier, 31)
 
-    def send_own(t, r, slot):
-        b = lane_of(r, 0)
-        push(buf.at[t, b, slot], buf.at[t, b, slot], ag_send.at[t, r, slot],
-             ag_recv.at[t, r, slot], dev(s, right))
-        push(buf.at[t, b, slot], buf.at[t, b, slot], ag_send.at[t, r, 2 + slot],
-             ag_recv.at[t, r, 2 + slot], dev(s, left))
+    def send_own(t, slot):
+        push(buf.at[t, lane, slot], buf.at[t, lane, slot], ag_send.at[t, 0, slot],
+             ag_recv.at[t, 0, slot], dev(s, right))
+        push(buf.at[t, lane, slot], buf.at[t, lane, slot], ag_send.at[t, 0, 2 + slot],
+             ag_recv.at[t, 0, 2 + slot], dev(s, left))
+
+    beyond = [dev(lax.rem(s + i - q + SEQ, SEQ), across) for i in range(2)]
+
+    def cross(t, b, i, k):
+        push(buf.at[t, b, i], buf.at[t, b, 1 - i], ag_send.at[t, 1, k + 1 - i],
+             ag_recv.at[t, 1, k + 1 - i], beyond[i])
 
     def send_roll(t, ref):
         before = lax.rem(s + SEQ - 1, SEQ)
@@ -162,42 +186,41 @@
         push(ref.at[pl.ds(HALF, HALF)], buf.at[t, lane, p], y_send.at[t, 1], y_recv.at[t, p],
              dev(s, across))
 
-    def own_ready(t):
+    def own_local(t):
+        blocks[t].wait()
+
         @pl.when(p == 0)
         def _():
             pltpu.make_async_copy(
                 (x_ref, g_ref)[t].at[pl.ds(0, HALF)], buf.at[t, lane, 0], local_sem.at[2 + t]
             ).wait()
 
+    def own_rolled(t):
         @pl.when(p == 1)
         def _():
             arrived(buf.at[t, lane, 1], roll_recv.at[t])
 
     send_roll(0, x_ref)
+    own_local(0)
+    send_own(0, 0)
     send_across(0, x_ref)
-    send_roll(1, g_ref)
-    send_across(1, g_ref)
+    own_rolled(0)
+    send_own(0, 1)
     push(wq_ref.at[:, 1 - c], wqb, w_send.at[0], w_recv.at[0], dev(s, sib))
-    push(wkvd_ref.at[:, 1 - c, :, pl.ds(0, 128)], wkvs, w_send.at[1], w_recv.at[1], dev(s, sib))
-    blocks[0].wait()
-    own_ready(0)
-    for slot in range(2):
-        send_own(0, 0, slot)
+    for j in range(LANES):
+        cols = pl.ds(pl.multiple_of((2 * j + 1 - c) * BLK, BLK), BLK)
+        push(kvt_ref.at[:, :, cols], wkv.at[j, pl.ds(0, 2), c], w_send.at[22 + j],
+             w_recv.at[22 + j], dev(s, sib))
     for j in range(LANES):
         cols = pl.ds(pl.multiple_of((2 * j + 1 - c) * BLK, BLK), BLK)
         push(wo_ref.at[:, cols], wob.at[j], w_send.at[2 + j], w_recv.at[2 + j], dev(s, sib))
-    blocks[1].wait()
-    own_ready(1)
-    for slot in range(2):
-        send_own(1, 0, slot)
-    weights[2].wait()
+    send_roll(1, g_ref)
     for d in range(1, LANES):
         push(up_ref, upb.at[lane, pl.ds(0, 16)], w_send.at[10 + d], w_recv.at[10 + d],
              dev(s, lax.rem(lane + d, LANES) * 2 + c))
     push(qup_ref.at[pl.ds(0, 16)], qups, w_send.at[18], w_recv.at[18], dev(s, sib))
     for k, peer in enumerate((sib, twin, twin_sib)):
-        push(kvup_ref.at[pl.ds(0, 32)], kvur.at[k], w_send.at[19 + k], w_recv.at[19 + k],
-             dev(s, peer))
+        push(kvup_ref, kvur.at[k], w_send.at[19 + k], w_recv.at[19 + k], dev(s, peer))
 
     def multiply(t, b):
         def rows(i, carry):
@@ -205,7 +228,7 @@
             if t == 0:
                 acc_q0[i] += dot(block, wqa[b])
                 acc_q1[i] += dot(block, wqb[b])
-                acc_kd[i] += dot(block, wkv[b])
+                acc_kd[i] += dot_nt(block, wkv[b].reshape(256, BLK))
             else:
                 acc_g0[i] += dot_nt(block, woa[b])
                 acc_g1[i] += dot_nt(block, wob[b])
@@ -231,8 +254,13 @@
              ag_recv.at[t, r, 5], dev(s, left))
 
     def sides_ready(t, r):
-        arrived(buf.at[t, lane_of(r, -1), 1], ag_recv.at[t, r, 1])
-        arrived(buf.at[t, lane_of(r, 1), 0], ag_recv.at[t, r, 2])
+        from_left, from_right = lane_of(r, -1), lane_of(r, 1)
+        arrived(buf.at[t, from_right, 0], ag_recv.at[t, r, 2])
+        if r == 0:
+            cross(t, from_right, 0, 2)
+        arrived(buf.at[t, from_left, 1], ag_recv.at[t, r, 1])
+        if r == 0:
+            cross(t, from_left, 1, 0)
 
     def far_ready(t, r):
         far = lane_of(r, 2)
@@ -241,46 +269,35 @@
 
     def across_ready(t):
         b = lane_of(1, 0)
-        for slot in range(2):
+        for slot, device, k in ((0, left, 2), (1, right, 1)):
             arrived(buf.at[t, b, slot], y_recv.at[t, slot])
-            send_own(t, 1, slot)
+            push(buf.at[t, b, slot], buf.at[t, b, slot], ag_send.at[t, 1, k],
+                 ag_recv.at[t, 1, k], dev(s, device))
 
     forward(0, 0)
+    sides_ready(0, 0)
     across_ready(0)
-    forward(1, 0)
-    for k in (0, 1):
-        weights[k].wait()
+    own_local(1)
+    send_own(1, 0)
+    send_across(1, g_ref)
+    own_rolled(1)
+    send_own(1, 1)
+    for copy in weights[0:9]:
+        copy.wait()
     arrived(wqb, w_recv.at[0])
-    arrived(wkvs, w_recv.at[1])
-
-    def join(j, carry):
-        wkv[j, :, 0:128] += wkvs[j]
-        return carry
-
-    lax.fori_loop(0, LANES, join, 0)
-    sides_ready(0, 0)
-    across_ready(1)
-    multiply(0, lane_of(0, 0))
+    for j in range(LANES):
+        arrived(wkv.at[j, pl.ds(0, 2), 1 - c], w_recv.at[22 + j])
+    multiply(0, lane)
     multiply_sides(0, 0)
-    sides_ready(1, 0)
-    for copy in weights[3:]:
-        copy.wait()
-    for j in range(LANES):
-        arrived(wob.at[j], w_recv.at[2 + j])
-    for d in range(1, LANES):
-        arrived(upb.at[lax.rem(lane - d + LANES, LANES), pl.ds(0, 16)], w_recv.at[10 + d])
-    multiply(1, lane_of(0, 0))
-    multiply_sides(1, 0)
+    multiply(0, lane_of(1, 0))
     forward(0, 1)
     far_ready(0, 0)
     multiply(0, lane_of(0, 2))
-    forward(1, 1)
-    multiply(0, lane_of(1, 0))
+    forward(1, 0)
+    sides_ready(1, 0)
+    across_ready(1)
     sides_ready(0, 1)
     multiply_sides(0, 1)
-    far_ready(1, 0)
-    multiply(1, lane_of(0, 2))
-    multiply(1, lane_of(1, 0))
     far_ready(0, 1)
     multiply(0, lane_of(1, 2))
 
@@ -293,14 +310,14 @@
     push(lip, lipr, m_send.at[3], m_recv.at[3], dev(s, sib))
     push(sq, sqr, m_send.at[4], m_recv.at[4], dev(s, sib))
 
-    sides_ready(1, 1)
-    multiply_sides(1, 1)
-    far_ready(1, 1)
-    multiply(1, lane_of(1, 2))
-    sg[...] = acc_g1[...].astype(BF16)
-    slg[...] = acc_lg[...].astype(BF16)
-    push(slg, slgr, m_send.at[5], m_recv.at[5], dev(s, sib))
-    push(sg, sgr, m_send.at[6], m_recv.at[6], dev(s, sib))
+    for copy in weights[9:]:
+        copy.wait()
+    for j in range(LANES):
+        arrived(wob.at[j], w_recv.at[2 + j])
+    for d in range(1, LANES):
+        arrived(upb.at[lax.rem(lane - d + LANES, LANES), pl.ds(0, 16)], w_recv.at[10 + d])
+    multiply(1, lane)
+    multiply_sides(1, 0)
 
     for k in range(3):
         arrived(kvur.at[k], w_recv.at[19 + k])
@@ -353,6 +370,8 @@
             return carry
 
         lax.fori_loop(0, 2, attend, 0)
+        if i == 0:
+            forward(1, 1)
     loti = jnp.concatenate(
         [
             dot_nt(od_ref[0:16, 0:128], att[0, i]) + dot_nt(od_ref[0:16, 128:256], att[1, i])
@@ -362,6 +381,18 @@
     )
     lot[...] = loti.astype(BF16)
     push(lot, lotr, m_send.at[7], m_recv.at[7], dev(s, sib))
+
+    far_ready(1, 0)
+    multiply(1, lane_of(0, 2))
+    multiply(1, lane_of(1, 0))
+    sides_ready(1, 1)
+    multiply_sides(1, 1)
+    far_ready(1, 1)
+    multiply(1, lane_of(1, 2))
+    sg[...] = acc_g1[...].astype(BF16)
+    slg[...] = acc_lg[...].astype(BF16)
+    push(slg, slgr, m_send.at[5], m_recv.at[5], dev(s, sib))
+    push(sg, sgr, m_send.at[6], m_recv.at[6], dev(s, sib))
 
     arrived(slgr, m_recv.at[5])
     arrived(sgr, m_recv.at[6])
@@ -426,7 +457,7 @@
         back_t.append(back.T[0:32, :])
 
     def dx_block(b, i):
-        return dot_nt(dq0[i], wqa[b]) + dot_nt(dq1[i], wqb[b]) + dot_nt(kb[i], wkv[b])
+        return dot_nt(dq0[i], wqa[b]) + dot_nt(dq1[i], wqb[b]) + dot(kb[i], wkv[b].reshape(256, BLK))
 
     def far_block(r):
         def one(i, carry):
@@ -437,29 +468,39 @@
         push(st.at[r, 0, 0], rsr.at[r, 0], rs_send.at[r, 0], rs_recv.at[r, 0], dev(s, right))
         push(st.at[r, 0, 1], rsr.at[r, 1], rs_send.at[r, 1], rs_recv.at[r, 1], dev(s, left))
 
-    def side_free(r):
-        st[r, 1, 1] = dx_block(lane_of(r, 1), 1).astype(BF16)
-        push(st.at[r, 1, 1], rsr.at[r, 3], rs_send.at[r, 3], rs_recv.at[r, 3], dev(s, right))
-        st[r, 2, 0] = dx_block(lane_of(r, -1), 0).astype(BF16)
-        push(st.at[r, 2, 0], rsr.at[r, 4], rs_send.at[r, 4], rs_recv.at[r, 4], dev(s, left))
-
-    def side_sum(r):
-        arrived(rsr.at[r, 0], rs_recv.at[r, 0])
-        st[r, 1, 0] = (dx_block(lane_of(r, 1), 0) + rsr[r, 0].astype(F32)).astype(BF16)
-        push(st.at[r, 1, 0], rsr.at[r, 2], rs_send.at[r, 2], rs_recv.at[r, 2], dev(s, right))
-        arrived(rsr.at[r, 1], rs_recv.at[r, 1])
-        st[r, 2, 1] = (dx_block(lane_of(r, -1), 1) + rsr[r, 1].astype(F32)).astype(BF16)
-        push(st.at[r, 2, 1], rsr.at[r, 5], rs_send.at[r, 5], rs_recv.at[r, 5], dev(s, left))
-
-    def own_block(r, i):
-        arrived(rsr.at[r, 2 + i], rs_recv.at[r, 2 + i])
-        arrived(rsr.at[r, 4 + i], rs_recv.at[r, 4 + i])
-        return dx_block(lane_of(r, 0), i) + rsr[r, 2 + i].astype(F32) + rsr[r, 4 + i].astype(F32)
+    def side_cross(d, i, extra):
+        k = 1 if d == 1 else 2
+        total = dx_block(lane_of(1, d), i)
+        arrived(rsr.at[1, extra], rs_recv.at[1, extra])
+        total += rsr[1, extra].astype(F32)
+        st[1, k, i] = total.astype(BF16)
+        slot = 2 * k + 1 - i
+        push(st.at[1, k, i], rsr.at[1, slot], rs_send.at[1, slot], rs_recv.at[1, slot], beyond[i])
+
+    def side_next(d, i, slot):
+        k = 1 if d == 1 else 2
+        st[1, k, i] = dx_block(lane_of(1, d), i).astype(BF16)
+        push(st.at[1, k, i], rsr.at[1, slot], rs_send.at[1, slot], rs_recv.at[1, slot],
+             dev(s, right if d == 1 else left))
+
+    def side_home(d, i, extra):
+        k = 1 if d == 1 else 2
+        slot = 2 * k + i
+        total = dx_block(lane_of(0, d), i)
+        if extra is not None:
+            arrived(rsr.at[0, extra], rs_recv.at[0, extra])
+            total += rsr[0, extra].astype(F32)
+        else:
+            arrived(rsr.at[1, slot], rs_recv.at[1, slot])
+            total += rsr[1, slot].astype(F32)
+        st[0, k, i] = total.astype(BF16)
+        push(st.at[0, k, i], rsr.at[0, slot], rs_send.at[0, slot], rs_recv.at[0, slot],
+             dev(s, right if d == 1 else left))
 
     far_block(1)
-    side_free(1)
+    side_next(1, 1, 2)
+    side_next(-1, 0, 5)
     far_block(0)
-    side_free(0)
 
     arrived(lotr, m_recv.at[7])
     back_full = jnp.concatenate(back_t, axis=1).astype(BF16)
@@ -477,11 +518,13 @@
         return carry
 
     lax.fori_loop(0, LANES, adapters, 0)
-    side_sum(1)
     for d in range(1, LANES):
         owner = lax.rem(lane + d, LANES)
         push(du.at[owner], r1buf.at[d - 1], s_send.at[0, d], s_recv.at[0, d],
              dev(s, owner * 2 + c))
+
+    side_cross(1, 0, 0)
+    side_cross(-1, 1, 1)
 
     low_t = jnp.concatenate([low[i].astype(F32).T[0:32] for i in range(2)], axis=1).astype(BF16)
     lg_t = jnp.concatenate([lgs[i].astype(F32).T[0:16] for i in range(2)], axis=1).astype(BF16)
@@ -495,7 +538,13 @@
         out_down += jnp.concatenate(
             [dot(lg_t[:, cols], att[0, i]), dot(lg_t[:, cols], att[1, i])], axis=1
         )
-    side_sum(0)
+    for i, slot in ((0, 5), (1, 2)):
+        total = dx_block(lane_of(1, 0), i)
+        arrived(rsr.at[1, slot], rs_recv.at[1, slot])
+        yst[i] = (total + rsr[1, slot].astype(F32)).astype(BF16)
+        half = i + p - 2 * i * p
+        push(yst.at[i], yrecv.at[half], y_send.at[2, i], y_recv.at[2, half],
+             dev(lax.rem(s + i * p, SEQ), across))
     lane_col = lax.broadcasted_iota(jnp.int32, (8, 128), 1)
     kv_grad = SCALE * jnp.where(lane_col < 64, kv_up[8:16], kv_up[16:24])
     alone = jnp.concatenate(
@@ -520,12 +569,8 @@
         owner = lax.rem(s + d, SEQ)
         push(pieces.at[owner], r2buf.at[d - 1], s_send.at[1, d], s_recv.at[1, d], dev(owner, h))
 
-    for i in range(2):
-        yst[i] = own_block(1, i).astype(BF16)
-        half = i + p - 2 * i * p
-        push(yst.at[i], yrecv.at[half], y_send.at[2, i], y_recv.at[2, half],
-             dev(lax.rem(s + i * p, SEQ), across))
-
+    side_home(1, 0, 0)
+    side_home(-1, 1, 1)
     mine = pieces[s].astype(F32)
     for d in range(1, SEQ):
         arrived(r2buf.at[d - 1], s_recv.at[1, d])
@@ -535,6 +580,26 @@
         push(agbuf.at[s], agbuf.at[s], s_send.at[2, d], s_recv.at[2, d],
              dev(lax.rem(s + d, SEQ), h))
 
+    side_home(1, 1, None)
+    side_home(-1, 0, None)
+    for d in range(1, SEQ):
+        arrived(agbuf.at[lax.rem(s - d + SEQ, SEQ)], s_recv.at[2, d])
+    for d in range(1, LANES):
+        push(agbuf.at[pl.ds(0, 8)], dbuf.at[lane, c], s_send.at[3, d], s_recv.at[3, d],
+             dev(s, lax.rem(lane + d, LANES) * 2 + c))
+    dbuf[lane, c] = agbuf[0:8]
+    for k in range(4):
+        cols = slice(k * 128, k * 128 + 128)
+        small_ref[0:8, cols] = agbuf[4 + k].astype(F32)[8:16]
+        small_ref[8:24, cols] = agbuf[8 + k].astype(F32)
+    kv_out = agbuf[8].astype(F32)[8:16]
+    small_ref[16:24, 0:64] = jnp.concatenate(
+        [
+            jnp.where(c == 0, kv_out[:, 0:32], kv_out[:, 32:64]),
+            jnp.where(c == 0, kv_out[:, 64:96], kv_out[:, 96:128]),
+        ],
+        axis=1,
+    )
     after = lax.rem(s + 1, SEQ)
 
     def send_back():
@@ -542,7 +607,11 @@
 
     rolled_sends.append(send_back)
     for i in (1, 0):
-        rown[i] = own_block(0, i)
+        total = dx_block(lane, i)
+        for k in (2, 4):
+            arrived(rsr.at[0, k + i], rs_recv.at[0, k + i])
+            total += rsr[0, k + i].astype(F32)
+        rown[i] = total
         if i == 1:
 
             @pl.when(p == 1)
@@ -550,20 +619,9 @@
                 rollst[...] = rown[1].astype(BF16)
                 send_back().start()
 
-    for d in range(1, SEQ):
-        arrived(agbuf.at[lax.rem(s - d + SEQ, SEQ)], s_recv.at[2, d])
-    for d in range(1, 16):
-        push(agbuf.at[pl.ds(0, 8)], dbuf.at[h], s_send.at[3, d], s_recv.at[3, d],
-             dev(s, lax.rem(h + d, 16)))
-    for k in range(4):
-        cols = slice(k * 128, k * 128 + 128)
-        oug_ref[:, cols] = agbuf[4 + k].astype(F32)[8:16]
-    for k in range(2):
-        cols = slice(k * 128, k * 128 + 128)
-        qg_ref[:, cols] = agbuf[8 + k].astype(F32)[0:8]
-        odg_ref[:, cols] = agbuf[10 + k].astype(F32)[0:8]
-    kvg_ref[...] = agbuf[8].astype(F32)[8:16]
-    dbuf[h] = agbuf[0:8]
+    for d in range(1, LANES):
+        arrived(dbuf.at[lax.rem(lane - d + LANES, LANES), c], s_recv.at[3, d])
+    push(dbuf.at[:, c], dbuf.at[:, c], s_send.at[3, 0], s_recv.at[3, 0], dev(s, sib))
 
     for half in range(2):
         arrived(yrecv.at[half], y_recv.at[2, half])
@@ -579,14 +637,13 @@
         dx_ref[HALF:ROWS, :] = (rown[0] + yrecv[1].astype(F32)).astype(BF16)
         dx_ref[0:HALF, :] = (rollrecv[...].astype(F32) + yrecv[0].astype(F32)).astype(BF16)
 
-    for d in range(1, 16):
-        arrived(dbuf.at[lax.rem(h - d + 16, 16)], s_recv.at[3, d])
+    arrived(dbuf.at[:, 1 - c], s_recv.at[3, 0])
 
     def place(j, carry):
         for k in range(4):
             cols = pl.ds(pl.multiple_of(j * BLK + k * 128, 128), 128)
-            dgrad_ref[0:16, cols] = dbuf[j, k].astype(F32)
-            dgrad_ref[16:24, cols] = dbuf[j, 4 + k].astype(F32)[0:8]
+            dgrad_ref[0:16, cols] = dbuf[j // 2, lax.rem(j, 2), k].astype(F32)
+            dgrad_ref[16:24, cols] = dbuf[j // 2, lax.rem(j, 2), 4 + k].astype(F32)[0:8]
         return carry
 
     lax.fori_loop(0, 16, place, 0)
@@ -618,26 +675,8 @@
     cos_wide = jnp.concatenate([cos, cos], axis=1).reshape(2, HALF, HEAD_SIZE)
     sin_wide = jnp.concatenate([-sin, sin], axis=1).reshape(2, HALF, HEAD_SIZE)
 
-    keys, values = key_value_weight[:, 0], key_value_weight[:, 1]
-    blank = jnp.zeros_like(keys)
-    placed = jnp.where(
-        c == 0,
-        jnp.concatenate([keys, blank, values, blank], axis=1),
-        jnp.concatenate([blank, keys, blank, values], axis=1),
-    )
-    down_t = adapter_down.reshape(3 * RANK, width).T
-    wkvd = jnp.concatenate(
-        [placed, down_t, jnp.zeros((width, 128 - 3 * RANK), BF16)], axis=1
-    ).reshape(LANES, 2, BLK, 256)
+    kvt = key_value_weight.transpose(1, 2, 0)
     wq = query_weight.reshape(LANES, 2, BLK, 256)
-
-    def tall(array, rows):
-        return jnp.pad(array, ((0, rows - array.shape[0]), (0, 0)))
-
-    column = lax.rem(h, 4) * 32
-    kvup = jnp.zeros((128, 256), BF16)
-    kvup = lax.dynamic_update_slice(kvup, key_value_up[:, 0], (8, column))
-    kvup = lax.dynamic_update_slice(kvup, key_value_up[:, 1], (16, 128 + column))
 
     vm = lambda *shape: pltpu.VMEM(shape, BF16)
     vf = lambda *shape: pltpu.VMEM(shape, F32)
@@ -645,17 +684,15 @@
     out_shape = [
         jax.ShapeDtypeStruct((ROWS, BLK), BF16),
         jax.ShapeDtypeStruct((3 * RANK, width), F32),
-        jax.ShapeDtypeStruct((RANK, 256), F32),
-        jax.ShapeDtypeStruct((RANK, 128), F32),
-        jax.ShapeDtypeStruct((RANK, 256), F32),
-        jax.ShapeDtypeStruct((RANK, BLK), F32),
+        jax.ShapeDtypeStruct((3 * RANK, BLK), F32),
     ]
     hbm = pl.BlockSpec(memory_space=pl.ANY)
     vmem = pl.BlockSpec(memory_space=pltpu.VMEM)
     scratch = [
         vm(2, LANES, 2, HALF, BLK), vm(LANES, BLK, 256), vm(LANES, BLK, 256),
-        vm(LANES, BLK, 256), vm(LANES, BLK, 128), vm(LANES, 256, BLK), vm(LANES, 256, BLK),
+        vm(LANES, 4, 2, 32, BLK), vm(LANES, 256, BLK), vm(LANES, 256, BLK),
         vm(LANES, 128, BLK), vm(16, 256), vm(3, 32, 256), vm(128, 256),
+        vm(128, 256), vm(32, 256), vm(128, 256), vm(16, BLK),
         vf(2, HALF, 256), vf(2, HALF, 256), vf(2, HALF, 256), vf(2, HALF, 256),
         vf(2, HALF, 256), vf(2, HALF, 128),
         vm(2, HALF, 256), vm(2, HALF, 256), vm(2, HALF, 128), vm(2, HALF, 128),
@@ -669,15 +706,15 @@
         vm(2, 3, 2, HALF, BLK), vm(2, 6, HALF, BLK), vf(2, HALF, BLK), vm(2, HALF, BLK),
         vm(2, HALF, BLK), vm(HALF, BLK), vm(HALF, BLK),
         vm(LANES, 32, BLK), vm(LANES - 1, 32, BLK), vm(16, 16, 128), vm(15, 16, 128),
-        vm(16, 16, 128), vm(16, 8, 16, 128),
-        dma(16), dma(22), dma(22), dma(2, 2, 6), dma(2, 2, 6), dma(3, 2), dma(3, 2),
+        vm(16, 16, 128), vm(LANES, 2, 8, 16, 128),
+        dma(21), dma(30), dma(30), dma(2, 2, 6), dma(2, 2, 6), dma(3, 2), dma(3, 2),
         dma(3), dma(3), dma(12), dma(12), dma(2, 6), dma(2, 6), dma(4, 16), dma(4, 16),
     ]
-    dx, dgrad, qg, kvg, odg, oug = pl.pallas_call(
+    dx, dgrad, small = pl.pallas_call(
         kernel,
         out_shape=out_shape,
-        in_specs=[hbm] * 5 + [vmem] * 3 + [hbm] + [vmem] * 2,
-        out_specs=[vmem] * 6,
+        in_specs=[hbm] * 5 + [vmem] * 7,
+        out_specs=[vmem] * 3,
         scratch_shapes=scratch,
         compiler_params=pltpu.CompilerParams(
             collective_id=0, has_side_effects=True, vmem_limit_bytes=56 * 1024 * 1024
@@ -686,17 +723,17 @@
             flops=9_000_000_000, bytes_accessed=20_000_000, transcendentals=400_000
         ),
     )(
-        normed, output_gradient, wq, wkvd, output_weight, tall(query_up, 128), kvup,
-        tall(output_down, 128), tall(output_up, 16), cos_wide, sin_wide,
+        normed, output_gradient, wq, kvt, output_weight, adapter_down.reshape(3 * RANK, width),
+        query_up, key_value_up.reshape(RANK, 64), output_down, output_up, cos_wide, sin_wide,
     )
-    kv_grad = jnp.stack(
-        [
-            lax.dynamic_slice_in_dim(kvg, c * 32, 32, 1),
-            lax.dynamic_slice_in_dim(kvg, 64 + c * 32, 32, 1),
-        ],
-        axis=1,
+    return (
+        dx,
+        dgrad.reshape(3, RANK, width),
+        small[8:16, 0:256],
+        small[16:24, 0:64].reshape(RANK, 2, 32),
+        small[8:16, 256:512],
+        small[0:8],
     )
-    return dx, dgrad.reshape(3, RANK, width), qg, kv_grad, odg, oug
 
 
 def solution(mesh):

time: 202 us -> 166 us (0.82)
  the two profiles are of different devices: /device:TPU:9 before, /device:TPU:48 now
where the time goes in v2:
time: 166 us; the launch traced here: 164 us
  Pallas kernels  152 us (92%)
  local copies, waits for them, and re-layouts  9.28 us (6%)
  other arithmetic  2.01 us (1%)
    pallas_call x1, Pallas kernels, body(): pl.pallas_call(kernel, out_shape=out_shape, in_specs=[hbm] * 5 + [vmem] *...  152 us
    unnamed x2, local copies, waits for them, and re-layouts  3.93 us

profile of v2, /device:TPU:48, one launch (start us, length us, event | category | flops | bytes accessed | tf_op | source)
XLA Modules:
  0.0 163.6 jit_solution(2292957237664947584)
XLA Ops:
  0.7 1.3 reshape.93.kvup_in
  2.0 1.0 fusion
  3.0 1.0 pad_maximum_fusion
  4.0 151.7 %shard_map.145 = (bf16[512,512]{1,0:T(8,128)(2,1)}, f32[24,8192]{1,0:T(8,128)}, f32[24,512]{1,0:T(8,128)}) custom-call(bf16[512,512]{1,0:T(8,128)(2,1)} %x_ref.1, bf16[512,512]{1,0:T(8,128)(2,1)} %g_ref.1, bf16[8,2,512,256]{3,2,1,0:T(8,128)(2,1)} %bitcast.5, bf16[2,32,8192]{2,1,0:T(8,128)(2,1)} %bitcast.6, bf16[256,8192]{1,0:T(8,128)(2,1)} %wo_ref.1, ...), custom_call_target="tpu_custom_call" | custom-call | flops 8999999488 | bytes 20000000 | tf_op jit(solution)/shard_map/pallas_call | solution.py:713
  155.7 0.7 slice.13
  156.4 0.7 reshape.95
  157.1 1.3 slice.15
  158.4 1.3 fusion.3
  159.7 1.9 %copy.18 = bf16[512,512]{1,0:T(8,128)(2,1)} copy(bf16[512,512]{1,0:T(8,128)(2,1)} %get-tuple-element.25) | data formatting | bytes 1048576
  161.6 2.1 %copy.19 = f32[3,8,8192]{2,1,0:T(8,128)} copy(f32[3,8,8192]{2,1,0:T(8,128)} %bitcast.4) | data formatting | bytes 1572864
  (2 shorter events, 0.0 us)

commit v3 on v2

--- a/solution.py
+++ b/solution.py
@@ -45,7 +45,7 @@
     probs, qs, ks, vs, att, gas, low, lgs, dkacc, dvacc,
     dq0, dq1, kb, lot, lotr, mown, moth, dkvr,
     st, rsr, rown, yst, yrecv, rollst, rollrecv,
-    du, r1buf, pieces, r2buf, agbuf, dbuf,
+    du, r1buf, al, alr, pieces, r2buf, tiles, eb,
     local_sem, w_send, w_recv, ag_send, ag_recv, y_send, y_recv, roll_send, roll_recv,
     m_send, m_recv, rs_send, rs_recv, s_send, s_recv,
 ):
@@ -63,6 +63,9 @@
     twin = h + 2 - 4 * a
     twin_sib = twin + 1 - 2 * c
     across = h + 8 - 16 * p
+    z = s // 2
+    k_lo = lax.rem(s, 2)
+    place_in_plane = k_lo * 8 + lane
 
     def dev(seq, head):
         return (seq, head)
@@ -92,17 +95,22 @@
         ).wait_recv()
 
     barrier = pltpu.get_barrier_semaphore()
+    def plane_peer(d):
+        m = lax.rem(place_in_plane + d, 16)
+        return m // 8, lax.rem(m, 8)
+
+    def column_peer(d):
+        return lax.rem(z + d, 8)
+
+    greeted = [dev(s, sib), dev(s, twin_sib)]
+    greeted += [dev(lax.rem(s + 2 * p - 1 + SEQ, SEQ), across)]
+    greeted += [dev(lax.rem(s + d, SEQ), h) for d in (1, SEQ - 1)]
     for d in range(1, 16):
-        pl.semaphore_signal(
-            barrier, inc=1, device_id=dev(s, lax.rem(h + d, 16)), device_id_type=MESH
-        )
-        pl.semaphore_signal(
-            barrier, inc=1, device_id=dev(lax.rem(s + d, SEQ), h), device_id_type=MESH
-        )
-    pl.semaphore_signal(
-        barrier, inc=1,
-        device_id=dev(lax.rem(s + 2 * p - 1 + SEQ, SEQ), across), device_id_type=MESH,
-    )
+        lo, j = plane_peer(d)
+        greeted.append(dev(z * 2 + lo, j * 2 + c))
+    greeted += [dev(column_peer(d) * 2 + k_lo, h) for d in range(1, 8)]
+    for device in greeted:
+        pl.semaphore_signal(barrier, inc=1, device_id=device, device_id_type=MESH)
 
     locals_ = []
 
@@ -153,7 +161,7 @@
         cols = pl.ds(pl.multiple_of((2 * j + c) * BLK, BLK), BLK)
         wkv[j, 2, 0] = jnp.concatenate([down_ref[:, cols], jnp.zeros((8, BLK), BF16)], axis=0)
 
-    pl.semaphore_wait(barrier, 31)
+    pl.semaphore_wait(barrier, len(greeted))
 
     def send_own(t, slot):
         push(buf.at[t, lane, slot], buf.at[t, lane, slot], ag_send.at[t, 0, slot],
@@ -277,25 +285,21 @@
     forward(0, 0)
     sides_ready(0, 0)
     across_ready(0)
-    own_local(1)
-    send_own(1, 0)
     send_across(1, g_ref)
-    own_rolled(1)
-    send_own(1, 1)
     for copy in weights[0:9]:
         copy.wait()
     arrived(wqb, w_recv.at[0])
     for j in range(LANES):
         arrived(wkv.at[j, pl.ds(0, 2), 1 - c], w_recv.at[22 + j])
     multiply(0, lane)
+    own_local(1)
+    own_rolled(1)
+    forward(0, 1)
+    send_own(1, 0)
     multiply_sides(0, 0)
     multiply(0, lane_of(1, 0))
-    forward(0, 1)
     far_ready(0, 0)
     multiply(0, lane_of(0, 2))
-    forward(1, 0)
-    sides_ready(1, 0)
-    across_ready(1)
     sides_ready(0, 1)
     multiply_sides(0, 1)
     far_ready(0, 1)
@@ -304,9 +308,9 @@
     sq[...] = acc_q1[...].astype(BF16)
     kvp[...] = acc_kd[:, :, 0:128].astype(BF16)
     lip[...] = acc_kd[:, :, 128:256].astype(BF16)
+    push(kvp, kvr.at[1], m_send.at[1], m_recv.at[1], dev(s, twin))
+    send_own(1, 1)
     push(kvp, kvr.at[0], m_send.at[0], m_recv.at[0], dev(s, sib))
-    push(kvp, kvr.at[1], m_send.at[1], m_recv.at[1], dev(s, twin))
-    push(kvp, kvr.at[2], m_send.at[2], m_recv.at[2], dev(s, twin_sib))
     push(lip, lipr, m_send.at[3], m_recv.at[3], dev(s, sib))
     push(sq, sqr, m_send.at[4], m_recv.at[4], dev(s, sib))
 
@@ -317,14 +321,14 @@
     for d in range(1, LANES):
         arrived(upb.at[lax.rem(lane - d + LANES, LANES), pl.ds(0, 16)], w_recv.at[10 + d])
     multiply(1, lane)
-    multiply_sides(1, 0)
 
     for k in range(3):
         arrived(kvur.at[k], w_recv.at[19 + k])
     arrived(qups, w_recv.at[18])
     kvf[0:32, :] = kvup_ref[0:32, :] + kvur[0] + kvur[1] + kvur[2]
+    arrived(kvr.at[1], m_recv.at[1])
+    push(kvr.at[1], kvr.at[2], m_send.at[2], m_recv.at[2], dev(s, sib))
     arrived(kvr.at[0], m_recv.at[0])
-    arrived(kvr.at[1], m_recv.at[1])
     arrived(kvr.at[2], m_recv.at[2])
     arrived(lipr, m_recv.at[3])
     arrived(sqr, m_recv.at[4])
@@ -371,7 +375,9 @@
 
         lax.fori_loop(0, 2, attend, 0)
         if i == 0:
-            forward(1, 1)
+            forward(1, 0)
+            sides_ready(1, 0)
+            across_ready(1)
     loti = jnp.concatenate(
         [
             dot_nt(od_ref[0:16, 0:128], att[0, i]) + dot_nt(od_ref[0:16, 128:256], att[1, i])
@@ -382,9 +388,11 @@
     lot[...] = loti.astype(BF16)
     push(lot, lotr, m_send.at[7], m_recv.at[7], dev(s, sib))
 
+    multiply_sides(1, 0)
+    multiply(1, lane_of(1, 0))
     far_ready(1, 0)
     multiply(1, lane_of(0, 2))
-    multiply(1, lane_of(1, 0))
+    forward(1, 1)
     sides_ready(1, 1)
     multiply_sides(1, 1)
     far_ready(1, 1)
@@ -429,7 +437,6 @@
         mown[i] = jnp.where(a == 0, low_side, high_side).astype(BF16)
         moth[i] = jnp.where(a == 0, high_side, low_side).astype(BF16)
     push(moth, dkvr.at[1], m_send.at[9], m_recv.at[9], dev(s, twin))
-    push(moth, dkvr.at[2], m_send.at[10], m_recv.at[10], dev(s, twin_sib))
     push(mown, dkvr.at[0], m_send.at[11], m_recv.at[11], dev(s, sib))
 
     kv_rows = kvf[0:32, :].astype(F32)
@@ -439,8 +446,9 @@
     kv_chip = jnp.concatenate([kv_chip, jnp.zeros((96, 128), BF16)], axis=0)
     sib_up = jnp.concatenate([qups[...], jnp.zeros((112, 256), BF16)], axis=0)
 
+    arrived(dkvr.at[1], m_recv.at[9])
+    push(dkvr.at[1], dkvr.at[2], m_send.at[10], m_recv.at[10], dev(s, sib))
     arrived(dq1, m_recv.at[8])
-    arrived(dkvr.at[1], m_recv.at[9])
     arrived(dkvr.at[2], m_recv.at[10])
     arrived(dkvr.at[0], m_recv.at[11])
     back_t = []
@@ -498,9 +506,6 @@
              dev(s, right if d == 1 else left))
 
     far_block(1)
-    side_next(1, 1, 2)
-    side_next(-1, 0, 5)
-    far_block(0)
 
     arrived(lotr, m_recv.at[7])
     back_full = jnp.concatenate(back_t, axis=1).astype(BF16)
@@ -514,17 +519,15 @@
         for i in range(2):
             cols = slice(i * HALF, i * HALF + HALF)
             total += dot(back_full[:, cols], buf[0, j, i]) + dot(out_full[:, cols], buf[1, j, i])
-        du[j] = total.astype(BF16)
+        du[j, 0] = total[0:16].astype(BF16)
+        du[j, 1] = total[16:32].astype(BF16)
         return carry
 
     lax.fori_loop(0, LANES, adapters, 0)
-    for d in range(1, LANES):
-        owner = lax.rem(lane + d, LANES)
-        push(du.at[owner], r1buf.at[d - 1], s_send.at[0, d], s_recv.at[0, d],
-             dev(s, owner * 2 + c))
-
-    side_cross(1, 0, 0)
-    side_cross(-1, 1, 1)
+    for d in range(1, 16):
+        lo, j = plane_peer(d)
+        push(du.at[j, lo], r1buf.at[d - 1], s_send.at[0, d], s_recv.at[0, d],
+             dev(z * 2 + lo, j * 2 + c))
 
     low_t = jnp.concatenate([low[i].astype(F32).T[0:32] for i in range(2)], axis=1).astype(BF16)
     lg_t = jnp.concatenate([lgs[i].astype(F32).T[0:16] for i in range(2)], axis=1).astype(BF16)
@@ -538,13 +541,6 @@
         out_down += jnp.concatenate(
             [dot(lg_t[:, cols], att[0, i]), dot(lg_t[:, cols], att[1, i])], axis=1
         )
-    for i, slot in ((0, 5), (1, 2)):
-        total = dx_block(lane_of(1, 0), i)
-        arrived(rsr.at[1, slot], rs_recv.at[1, slot])
-        yst[i] = (total + rsr[1, slot].astype(F32)).astype(BF16)
-        half = i + p - 2 * i * p
-        push(yst.at[i], yrecv.at[half], y_send.at[2, i], y_recv.at[2, half],
-             dev(lax.rem(s + i * p, SEQ), across))
     lane_col = lax.broadcasted_iota(jnp.int32, (8, 128), 1)
     kv_grad = SCALE * jnp.where(lane_col < 64, kv_up[8:16], kv_up[16:24])
     alone = jnp.concatenate(
@@ -554,52 +550,66 @@
         ],
         axis=0,
     ).astype(BF16)
-    for k in range(4):
-        pieces[8 + k] = alone[:, k * 128 : k * 128 + 128]
-        pieces[12 + k] = jnp.zeros((16, 128), BF16)
-    shared = du[lane].astype(F32)
-    for d in range(1, LANES):
+    al[0] = alone[:, 0:256]
+    al[1] = alone[:, 256:512]
+    push(al.at[1 - k_lo], alr, s_send.at[4, 1], s_recv.at[4, 1], dev(z * 2 + 1 - k_lo, h))
+    side_next(1, 1, 2)
+    side_next(-1, 0, 5)
+    far_block(0)
+    side_cross(1, 0, 0)
+    side_cross(-1, 1, 1)
+
+    shared = du[lane, k_lo].astype(F32)
+    for d in range(1, 16):
         arrived(r1buf.at[d - 1], s_recv.at[0, d])
         shared += r1buf[d - 1].astype(F32)
-    shared = shared.astype(BF16)
-    for g in range(2):
-        for k in range(4):
-            pieces[4 * g + k] = shared[16 * g : 16 * g + 16, k * 128 : k * 128 + 128]
-    for d in range(1, SEQ):
-        owner = lax.rem(s + d, SEQ)
-        push(pieces.at[owner], r2buf.at[d - 1], s_send.at[1, d], s_recv.at[1, d], dev(owner, h))
-
+    arrived(alr, s_recv.at[4, 1])
+    single = al[k_lo].astype(F32) + alr[...].astype(F32)
+    for k in range(8):
+        r, g = k // 4, k % 4
+        pieces[k, 0] = shared[8 * r : 8 * r + 8, g * 128 : g * 128 + 128]
+        r, g = k // 2, k % 2
+        if k < 4:
+            pieces[k, 1] = single[8 * r : 8 * r + 8, g * 128 : g * 128 + 128]
+        else:
+            pieces[k, 1] = jnp.zeros((8, 128), F32)
+    for d in range(1, 8):
+        owner = column_peer(d)
+        push(pieces.at[owner], r2buf.at[d - 1], s_send.at[1, d], s_recv.at[1, d],
+             dev(owner * 2 + k_lo, h))
+    mine = pieces[z]
+    for d in range(1, 8):
+        arrived(r2buf.at[d - 1], s_recv.at[1, d])
+        mine += r2buf[d - 1]
+    tiles[place_in_plane] = mine[0]
+    for d in range(1, 16):
+        lo, j = plane_peer(d)
+        push(tiles.at[place_in_plane], tiles.at[place_in_plane], s_send.at[2, d],
+             s_recv.at[2, d], dev(z * 2 + lo, j * 2 + c))
+    tiles[16 + k_lo] = mine[1]
+    push(tiles.at[16 + k_lo], tiles.at[16 + k_lo], s_send.at[4, 2], s_recv.at[4, 2],
+         dev(z * 2 + 1 - k_lo, h))
+
+    for i, slot in ((0, 5), (1, 2)):
+        total = dx_block(lane_of(1, 0), i)
+        arrived(rsr.at[1, slot], rs_recv.at[1, slot])
+        yst[i] = (total + rsr[1, slot].astype(F32)).astype(BF16)
+        half = i + p - 2 * i * p
+        push(yst.at[i], yrecv.at[half], y_send.at[2, i], y_recv.at[2, half],
+             dev(lax.rem(s + i * p, SEQ), across))
     side_home(1, 0, 0)
     side_home(-1, 1, 1)
-    mine = pieces[s].astype(F32)
-    for d in range(1, SEQ):
-        arrived(r2buf.at[d - 1], s_recv.at[1, d])
-        mine += r2buf[d - 1].astype(F32)
-    agbuf[s] = mine.astype(BF16)
-    for d in range(1, SEQ):
-        push(agbuf.at[s], agbuf.at[s], s_send.at[2, d], s_recv.at[2, d],
-             dev(lax.rem(s + d, SEQ), h))
-
+    for d in range(1, 16):
+        m = lax.rem(place_in_plane - d + 16, 16)
+        arrived(tiles.at[m], s_recv.at[2, d])
+    arrived(tiles.at[17 - k_lo], s_recv.at[4, 2])
+    for k in range(9):
+        eb[c, z, k] = jnp.concatenate([tiles[2 * k], tiles[2 * k + 1]], axis=0).astype(BF16)
+    for d in range(1, 8):
+        push(eb.at[c, z], eb.at[c, z], s_send.at[3, d], s_recv.at[3, d],
+             dev(column_peer(d) * 2 + k_lo, h))
     side_home(1, 1, None)
     side_home(-1, 0, None)
-    for d in range(1, SEQ):
-        arrived(agbuf.at[lax.rem(s - d + SEQ, SEQ)], s_recv.at[2, d])
-    for d in range(1, LANES):
-        push(agbuf.at[pl.ds(0, 8)], dbuf.at[lane, c], s_send.at[3, d], s_recv.at[3, d],
-             dev(s, lax.rem(lane + d, LANES) * 2 + c))
-    dbuf[lane, c] = agbuf[0:8]
-    for k in range(4):
-        cols = slice(k * 128, k * 128 + 128)
-        small_ref[0:8, cols] = agbuf[4 + k].astype(F32)[8:16]
-        small_ref[8:24, cols] = agbuf[8 + k].astype(F32)
-    kv_out = agbuf[8].astype(F32)[8:16]
-    small_ref[16:24, 0:64] = jnp.concatenate(
-        [
-            jnp.where(c == 0, kv_out[:, 0:32], kv_out[:, 32:64]),
-            jnp.where(c == 0, kv_out[:, 64:96], kv_out[:, 96:128]),
-        ],
-        axis=1,
-    )
     after = lax.rem(s + 1, SEQ)
 
     def send_back():
@@ -619,9 +629,26 @@
                 rollst[...] = rown[1].astype(BF16)
                 send_back().start()
 
-    for d in range(1, LANES):
-        arrived(dbuf.at[lax.rem(lane - d + LANES, LANES), c], s_recv.at[3, d])
-    push(dbuf.at[:, c], dbuf.at[:, c], s_send.at[3, 0], s_recv.at[3, 0], dev(s, sib))
+    for d in range(1, 8):
+        arrived(eb.at[c, lax.rem(z - d + 8, 8)], s_recv.at[3, d])
+    push(eb.at[c], eb.at[c], s_send.at[4, 0], s_recv.at[4, 0], dev(s, sib))
+    for g in range(4):
+        cols = slice(g * 128, g * 128 + 128)
+        pair = eb[c, 4 + g, 4 + lane // 2].astype(F32)
+        small_ref[0:8, cols] = jnp.where(lax.rem(lane, 2) == 0, pair[0:8], pair[8:16])
+    for g in range(2):
+        pair = eb[c, g, 8].astype(F32)
+        small_ref[8:16, g * 128 : g * 128 + 128] = pair[0:8]
+        small_ref[8:16, 256 + g * 128 : 384 + g * 128] = pair[8:16]
+    kv_out = eb[c, 2, 8].astype(F32)[0:8]
+    small_ref[16:24, :] = jnp.zeros((8, BLK), F32)
+    small_ref[16:24, 0:64] = jnp.concatenate(
+        [
+            jnp.where(c == 0, kv_out[:, 0:32], kv_out[:, 32:64]),
+            jnp.where(c == 0, kv_out[:, 64:96], kv_out[:, 96:128]),
+        ],
+        axis=1,
+    )
 
     for half in range(2):
         arrived(yrecv.at[half], y_recv.at[2, half])
@@ -637,16 +664,20 @@
         dx_ref[HALF:ROWS, :] = (rown[0] + yrecv[1].astype(F32)).astype(BF16)
         dx_ref[0:HALF, :] = (rollrecv[...].astype(F32) + yrecv[0].astype(F32)).astype(BF16)
 
-    arrived(dbuf.at[:, 1 - c], s_recv.at[3, 0])
+    arrived(eb.at[1 - c], s_recv.at[4, 0])
 
     def place(j, carry):
-        for k in range(4):
-            cols = pl.ds(pl.multiple_of(j * BLK + k * 128, 128), 128)
-            dgrad_ref[0:16, cols] = dbuf[j // 2, lax.rem(j, 2), k].astype(F32)
-            dgrad_ref[16:24, cols] = dbuf[j // 2, lax.rem(j, 2), 4 + k].astype(F32)[0:8]
+        for core in range(2):
+            for g in range(4):
+                cols = pl.ds(pl.multiple_of((2 * j + core) * BLK + g * 128, 128), 128)
+                for r in range(3):
+                    pair = eb[core, r % 2 * 4 + g, r // 2 * 4 + j // 2].astype(F32)
+                    dgrad_ref[8 * r : 8 * r + 8, cols] = jnp.where(
+                        lax.rem(j, 2) == 0, pair[0:8], pair[8:16]
+                    )
         return carry
 
-    lax.fori_loop(0, 16, place, 0)
+    lax.fori_loop(0, LANES, place, 0)
 
     for copy in sends:
         copy.wait_send()
@@ -655,6 +686,17 @@
     def _():
         for copy in rolled_sends:
             copy().wait_send()
+
+
+def finish(dx_ref, dgrad_ref, small_ref, out_dx, out_down, out_qg, out_kvg, out_odg, out_oug):
+    out_dx[...] = dx_ref[...]
+    for r in range(3):
+        out_down[r] = dgrad_ref[r * RANK : (r + 1) * RANK, :]
+    out_qg[...] = small_ref[8:16, 0:256]
+    out_odg[...] = small_ref[8:16, 256:512]
+    out_oug[...] = small_ref[0:8, :]
+    out_kvg[:, 0, :] = small_ref[16:24, 0:32]
+    out_kvg[:, 1, :] = small_ref[16:24, 32:64]
 
 
 def body(normed, output_gradient, query_weight, key_value_weight, output_weight,
@@ -705,10 +747,10 @@
         vm(2, HALF, 128), vm(2, HALF, 128), vm(3, 2, HALF, 128),
         vm(2, 3, 2, HALF, BLK), vm(2, 6, HALF, BLK), vf(2, HALF, BLK), vm(2, HALF, BLK),
         vm(2, HALF, BLK), vm(HALF, BLK), vm(HALF, BLK),
-        vm(LANES, 32, BLK), vm(LANES - 1, 32, BLK), vm(16, 16, 128), vm(15, 16, 128),
-        vm(16, 16, 128), vm(LANES, 2, 8, 16, 128),
+        vm(LANES, 2, 16, BLK), vm(15, 16, BLK), vm(2, 16, 256), vm(16, 256), vf(8, 2, 8, 128),
+        vf(7, 2, 8, 128), vf(18, 8, 128), vm(2, 8, 9, 16, 128),
         dma(21), dma(30), dma(30), dma(2, 2, 6), dma(2, 2, 6), dma(3, 2), dma(3, 2),
-        dma(3), dma(3), dma(12), dma(12), dma(2, 6), dma(2, 6), dma(4, 16), dma(4, 16),
+        dma(3), dma(3), dma(12), dma(12), dma(2, 6), dma(2, 6), dma(5, 16), dma(5, 16),
     ]
     dx, dgrad, small = pl.pallas_call(
         kernel,
@@ -726,13 +768,20 @@
         normed, output_gradient, wq, kvt, output_weight, adapter_down.reshape(3 * RANK, width),
         query_up, key_value_up.reshape(RANK, 64), output_down, output_up, cos_wide, sin_wide,
     )
-    return (
-        dx,
-        dgrad.reshape(3, RANK, width),
-        small[8:16, 0:256],
-        small[16:24, 0:64].reshape(RANK, 2, 32),
-        small[8:16, 256:512],
-        small[0:8],
+    return tuple(
+        pl.pallas_call(
+            finish,
+            out_shape=[
+                jax.ShapeDtypeStruct((ROWS, BLK), BF16),
+                jax.ShapeDtypeStruct((3, RANK, width), F32),
+                jax.ShapeDtypeStruct((RANK, 256), F32),
+                jax.ShapeDtypeStruct((RANK, 2, 32), F32),
+                jax.ShapeDtypeStruct((RANK, 256), F32),
+                jax.ShapeDtypeStruct((RANK, BLK), F32),
+            ],
+            in_specs=[vmem] * 3,
+            out_specs=[vmem] * 6,
+        )(dx, dgrad, small)
     )
 
 

time: 166 us -> 150 us (0.904)
  Pallas kernels: 152 us -> 144 us
  local copies, waits for them, and re-layouts: 9.28 us -> 1.35 us
    pallas_call x1, Pallas kernels: 152 us -> 141 us  [body(): pl.pallas_call(kernel, out_shape=out_shape, in_specs=[hbm] * 5 + [vmem] *...]
    unnamed x2 -> x0, local copies, waits for them, and re-layouts: 3.93 us -> none
    slice x3 -> x0, local copies, waits for them, and re-layouts: 3.32 us -> none  [the longest x1 1.32 us: body(): small[0:8]]
    pallas_call x0 -> x1, Pallas kernels: none -> 2.4 us  [body(): pl.pallas_call(finish, out_shape=[jax.ShapeDtypeStruct((ROWS, BLK), BF16)...]
where the time goes in v3:
time: 150 us; the launch traced here: 148 us
  Pallas kernels  144 us (96%)
  other arithmetic  2.01 us (1%)
    pallas_call x1, Pallas kernels, body(): pl.pallas_call(kernel, out_shape=out_shape, in_specs=[hbm] * 5 + [vmem] *...  141 us

profile of v3, /device:TPU:48, one launch (start us, length us, event | category | flops | bytes accessed | tf_op | source)
XLA Modules:
  0.0 147.6 jit_solution(14227277436356378409)
XLA Ops:
  0.7 1.3 reshape.87.kvup_in
  2.0 1.0 fusion
  3.0 1.0 pad_maximum_fusion
  4.0 141.2 %shard_map.145 = (bf16[512,512]{1,0:T(8,128)(2,1)}, f32[24,8192]{1,0:T(8,128)}, f32[24,512]{1,0:T(8,128)}) custom-call(bf16[512,512]{1,0:T(8,128)(2,1)} %x_ref.1, bf16[512,512]{1,0:T(8,128)(2,1)} %g_ref.1, bf16[8,2,512,256]{3,2,1,0:T(8,128)(2,1)} %bitcast.3, bf16[2,32,8192]{2,1,0:T(8,128)(2,1)} %bitcast.4, bf16[256,8192]{1,0:T(8,128)(2,1)} %wo_ref.1, ...), custom_call_target="tpu_custom_call" | custom-call | flops 8999999488 | bytes 20000000 | tf_op jit(solution)/shard_map/pallas_call | solution.py:755
  145.2 2.4 %shard_map.146 = (bf16[512,512]{1,0:T(8,128)(2,1)}, f32[3,8,8192]{2,1,0:T(8,128)}, f32[8,256]{1,0:T(8,128)}, f32[8,2,32]{2,1,0:T(2,128)}, f32[8,256]{1,0:T(8,128)}, /*index=5*/f32[8,512]{1,0:T(8,128)}) custom-call(bf16[512,512]{1,0:T(8,128)(2,1)} %get-tuple-element.9.dx_ref, f32[24,8192]{1,0:T(8,128)} %get-tuple-element.10.dgrad_ref, ...), custom_call_target="tpu_custom_call" | custom-call | tf_op jit(solution)/shard_map/pallas_call | solution.py:772
  (2 shorter events, 0.0 us)

commit v4 on v3

--- a/solution.py
+++ b/solution.py
@@ -37,15 +37,15 @@
 
 
 def kernel(
-    x_ref, g_ref, wq_ref, kvt_ref, wo_ref, down_ref, qup_in, kvup_in, od_in, up_in, cos_ref, sin_ref,
+    x_ref, g_ref, wq_ref, kvt_ref, wo_ref, down_ref, qup_in, kvup_in, od_in, up_in, cos_in, sin_in,
     dx_ref, dgrad_ref, small_ref,
-    buf, wqa, wqb, wkv, woa, wob, upb, qups, kvur, kvf, qup_ref, kvup_ref, od_ref, up_ref,
+    buf, wqa, wqb, wkv, woa, wob, upb, qups, kvur, kvf, qup_ref, kvup_ref, od_ref, up_ref, cos_ref, sin_ref,
     acc_q0, acc_q1, acc_kd, acc_g0, acc_g1, acc_lg,
     sq, sqr, lip, lipr, kvp, kvr, sg, sgr, slg, slgr,
     probs, qs, ks, vs, att, gas, low, lgs, dkacc, dvacc,
     dq0, dq1, kb, lot, lotr, mown, moth, dkvr,
     st, rsr, rown, yst, yrecv, rollst, rollrecv,
-    du, r1buf, al, alr, pieces, r2buf, tiles, eb,
+    ups, du, r1buf, al, alr, pieces, r2buf, tiles, eb,
     local_sem, w_send, w_recv, ag_send, ag_recv, y_send, y_recv, roll_send, roll_recv,
     m_send, m_recv, rs_send, rs_recv, s_send, s_recv,
 ):
@@ -146,10 +146,14 @@
     od_ref[...] = jnp.concatenate([od_in[...], jnp.zeros((120, 256), BF16)], axis=0)
     up_ref[...] = jnp.concatenate([up_in[...], jnp.zeros((8, BLK), BF16)], axis=0)
     upb[lane, 0:16, :] = up_ref[...]
+    for i in range(2):
+        cos_ref[i] = jnp.concatenate([cos_in[i], cos_in[i]], axis=1)
+        sin_ref[i] = jnp.concatenate([-sin_in[i], sin_in[i]], axis=1)
     source = lax.broadcasted_iota(jnp.int32, (64, 256), 0)
     target = lax.broadcasted_iota(jnp.int32, (64, 256), 1)
     goal = source + lax.rem(h, 4) * 32 + jnp.where(source < 32, 0, 96)
-    spread = dot(kvup_in[...], jnp.where(target == goal, 1.0, 0.0).astype(BF16))
+    goals = jnp.where(target == goal, 1.0, 0.0).astype(BF16)
+    spread = dot(kvup_in[:, 0, :], goals[0:32]) + dot(kvup_in[:, 1, :], goals[32:64])
     column = lax.broadcasted_iota(jnp.int32, (8, 256), 1)
     none = jnp.zeros((8, 256), F32)
     kvup_ref[...] = jnp.concatenate(
@@ -222,7 +226,6 @@
     for j in range(LANES):
         cols = pl.ds(pl.multiple_of((2 * j + 1 - c) * BLK, BLK), BLK)
         push(wo_ref.at[:, cols], wob.at[j], w_send.at[2 + j], w_recv.at[2 + j], dev(s, sib))
-    send_roll(1, g_ref)
     for d in range(1, LANES):
         push(up_ref, upb.at[lane, pl.ds(0, 16)], w_send.at[10 + d], w_recv.at[10 + d],
              dev(s, lax.rem(lane + d, LANES) * 2 + c))
@@ -285,6 +288,7 @@
     forward(0, 0)
     sides_ready(0, 0)
     across_ready(0)
+    send_roll(1, g_ref)
     send_across(1, g_ref)
     for copy in weights[0:9]:
         copy.wait()
@@ -293,9 +297,10 @@
         arrived(wkv.at[j, pl.ds(0, 2), 1 - c], w_recv.at[22 + j])
     multiply(0, lane)
     own_local(1)
+    send_own(1, 0)
+    forward(0, 1)
     own_rolled(1)
-    forward(0, 1)
-    send_own(1, 0)
+    send_own(1, 1)
     multiply_sides(0, 0)
     multiply(0, lane_of(1, 0))
     far_ready(0, 0)
@@ -309,7 +314,6 @@
     kvp[...] = acc_kd[:, :, 0:128].astype(BF16)
     lip[...] = acc_kd[:, :, 128:256].astype(BF16)
     push(kvp, kvr.at[1], m_send.at[1], m_recv.at[1], dev(s, twin))
-    send_own(1, 1)
     push(kvp, kvr.at[0], m_send.at[0], m_recv.at[0], dev(s, sib))
     push(lip, lipr, m_send.at[3], m_recv.at[3], dev(s, sib))
     push(sq, sqr, m_send.at[4], m_recv.at[4], dev(s, sib))
@@ -321,6 +325,9 @@
     for d in range(1, LANES):
         arrived(upb.at[lax.rem(lane - d + LANES, LANES), pl.ds(0, 16)], w_recv.at[10 + d])
     multiply(1, lane)
+    forward(1, 0)
+    sides_ready(1, 0)
+    across_ready(1)
 
     for k in range(3):
         arrived(kvur.at[k], w_recv.at[19 + k])
@@ -374,10 +381,6 @@
             return carry
 
         lax.fori_loop(0, 2, attend, 0)
-        if i == 0:
-            forward(1, 0)
-            sides_ready(1, 0)
-            across_ready(1)
     loti = jnp.concatenate(
         [
             dot_nt(od_ref[0:16, 0:128], att[0, i]) + dot_nt(od_ref[0:16, 128:256], att[1, i])
@@ -416,6 +419,27 @@
     lax.fori_loop(0, 2, cotangent, 0)
     dkacc[...] = jnp.zeros(dkacc.shape, F32)
     dvacc[...] = jnp.zeros(dvacc.shape, F32)
+
+    def split_columns(kind, halves):
+        for message, side in ((mown, a), (moth, 1 - a)):
+            low_side = jnp.concatenate([half[:, 0:64] for half in halves], axis=1)
+            high_side = jnp.concatenate([half[:, 64:128] for half in halves], axis=1)
+            message[kind] = jnp.where(side == 0, low_side, high_side).astype(BF16)
+        push(moth.at[kind], dkvr.at[1, kind], m_send.at[9 + 3 * kind], m_recv.at[9 + 3 * kind],
+             dev(s, twin))
+        push(mown.at[kind], dkvr.at[0, kind], m_send.at[11 + 3 * kind],
+             m_recv.at[11 + 3 * kind], dev(s, sib))
+
+    def pass_on(kind):
+        arrived(dkvr.at[1, kind], m_recv.at[9 + 3 * kind])
+        push(dkvr.at[1, kind], dkvr.at[2, kind], m_send.at[10 + 3 * kind],
+             m_recv.at[10 + 3 * kind], dev(s, sib))
+
+    for i in range(2):
+        keys = (i + 1) * HALF
+        for hd in range(2):
+            dvacc[0:keys, :] += dot_tn(probs[hd, i, :, 0:keys].astype(BF16), gas[hd, i])
+    split_columns(1, [dvacc[0:HALF, :], dvacc[HALF:ROWS, :]])
     for i in range(2):
         keys = (i + 1) * HALF
         for hd in range(2):
@@ -426,18 +450,24 @@
             dq = INV_ROOT * dot(ds, ks[0:keys, :])
             dq0[i, :, hd * 128 : hd * 128 + 128] = unrotate(dq, i).astype(BF16)
             dkacc[0:keys, :] += dot_tn(ds, qs[hd, i])
-            dvacc[0:keys, :] += dot_tn(full.astype(BF16), gas[hd, i])
     push(dq0, dq1, m_send.at[8], m_recv.at[8], dev(s, sib))
-    for i in range(2):
-        rows = slice(i * HALF, i * HALF + HALF)
-        dk = unrotate(INV_ROOT * dkacc[rows, :], i)
-        dv = dvacc[rows, :]
-        low_side = jnp.concatenate([dk[:, 0:64], dv[:, 0:64]], axis=1)
-        high_side = jnp.concatenate([dk[:, 64:128], dv[:, 64:128]], axis=1)
-        mown[i] = jnp.where(a == 0, low_side, high_side).astype(BF16)
-        moth[i] = jnp.where(a == 0, high_side, low_side).astype(BF16)
-    push(moth, dkvr.at[1], m_send.at[9], m_recv.at[9], dev(s, twin))
-    push(mown, dkvr.at[0], m_send.at[11], m_recv.at[11], dev(s, sib))
+    split_columns(
+        0,
+        [unrotate(INV_ROOT * dkacc[i * HALF : i * HALF + HALF, :], i) for i in range(2)],
+    )
+    pass_on(1)
+
+    arrived(lotr, m_recv.at[7])
+    low_out = (SCALE * (loti + lotr[...].astype(F32))).astype(BF16)
+
+    def out_up(j, carry):
+        total = jnp.zeros((16, BLK), F32)
+        for i in range(2):
+            total += dot(low_out[:, i * HALF : i * HALF + HALF], buf[1, j, i])
+        ups[j] = total[0:8]
+        return carry
+
+    lax.fori_loop(0, LANES, out_up, 0)
 
     kv_rows = kvf[0:32, :].astype(F32)
     kv_low = jnp.concatenate([kv_rows[:, 0:64], kv_rows[:, 128:192]], axis=1)
@@ -446,16 +476,21 @@
     kv_chip = jnp.concatenate([kv_chip, jnp.zeros((96, 128), BF16)], axis=0)
     sib_up = jnp.concatenate([qups[...], jnp.zeros((112, 256), BF16)], axis=0)
 
-    arrived(dkvr.at[1], m_recv.at[9])
-    push(dkvr.at[1], dkvr.at[2], m_send.at[10], m_recv.at[10], dev(s, sib))
+    pass_on(0)
     arrived(dq1, m_recv.at[8])
-    arrived(dkvr.at[2], m_recv.at[10])
-    arrived(dkvr.at[0], m_recv.at[11])
+    for kind in (1, 0):
+        arrived(dkvr.at[2, kind], m_recv.at[10 + 3 * kind])
+        arrived(dkvr.at[0, kind], m_recv.at[11 + 3 * kind])
     back_t = []
     for i in range(2):
-        total = (
-            mown[i].astype(F32) + dkvr[0, i].astype(F32)
-            + dkvr[1, i].astype(F32) + dkvr[2, i].astype(F32)
+        cols = slice(i * 64, i * 64 + 64)
+        total = jnp.concatenate(
+            [
+                mown[kind].astype(F32)[:, cols] + dkvr[0, kind].astype(F32)[:, cols]
+                + dkvr[1, kind].astype(F32)[:, cols] + dkvr[2, kind].astype(F32)[:, cols]
+                for kind in range(2)
+            ],
+            axis=1,
         ).astype(BF16)
         back = SCALE * (
             dot_nt(dq0[i], qup_ref[...]) + dot_nt(dq1[i], sib_up) + dot_nt(total, kv_chip)
@@ -507,20 +542,14 @@
 
     far_block(1)
 
-    arrived(lotr, m_recv.at[7])
     back_full = jnp.concatenate(back_t, axis=1).astype(BF16)
-    low_out = (SCALE * (loti + lotr[...].astype(F32))).astype(BF16)
-    out_full = jnp.concatenate(
-        [jnp.zeros((16, ROWS), BF16), jnp.zeros((8, ROWS), BF16), low_out[0:8]], axis=0
-    )
 
     def adapters(j, carry):
         total = jnp.zeros((32, BLK), F32)
         for i in range(2):
-            cols = slice(i * HALF, i * HALF + HALF)
-            total += dot(back_full[:, cols], buf[0, j, i]) + dot(out_full[:, cols], buf[1, j, i])
+            total += dot(back_full[:, i * HALF : i * HALF + HALF], buf[0, j, i])
         du[j, 0] = total[0:16].astype(BF16)
-        du[j, 1] = total[16:32].astype(BF16)
+        du[j, 1] = jnp.concatenate([total[16:24], ups[j]], axis=0).astype(BF16)
         return carry
 
     lax.fori_loop(0, LANES, adapters, 0)
@@ -714,8 +743,8 @@
     frequency = ROPE_BASE ** (-jnp.arange(half_dim, dtype=F32) * 2.0 / HEAD_SIZE)
     angles = positions[:, None] * frequency[None, :]
     cos, sin = jnp.cos(angles), jnp.sin(angles)
-    cos_wide = jnp.concatenate([cos, cos], axis=1).reshape(2, HALF, HEAD_SIZE)
-    sin_wide = jnp.concatenate([-sin, sin], axis=1).reshape(2, HALF, HEAD_SIZE)
+    cos = cos.reshape(2, HALF, half_dim)
+    sin = sin.reshape(2, HALF, half_dim)
 
     kvt = key_value_weight.transpose(1, 2, 0)
     wq = query_weight.reshape(LANES, 2, BLK, 256)
@@ -734,7 +763,8 @@
         vm(2, LANES, 2, HALF, BLK), vm(LANES, BLK, 256), vm(LANES, BLK, 256),
         vm(LANES, 4, 2, 32, BLK), vm(LANES, 256, BLK), vm(LANES, 256, BLK),
         vm(LANES, 128, BLK), vm(16, 256), vm(3, 32, 256), vm(128, 256),
-        vm(128, 256), vm(32, 256), vm(128, 256), vm(16, BLK),
+        vm(128, 256), vm(32, 256), vm(128, 256), vm(16, BLK), vf(2, HALF, HEAD_SIZE),
+        vf(2, HALF, HEAD_SIZE),
         vf(2, HALF, 256), vf(2, HALF, 256), vf(2, HALF, 256), vf(2, HALF, 256),
         vf(2, HALF, 256), vf(2, HALF, 128),
         vm(2, HALF, 256), vm(2, HALF, 256), vm(2, HALF, 128), vm(2, HALF, 128),
@@ -747,10 +777,10 @@
         vm(2, HALF, 128), vm(2, HALF, 128), vm(3, 2, HALF, 128),
         vm(2, 3, 2, HALF, BLK), vm(2, 6, HALF, BLK), vf(2, HALF, BLK), vm(2, HALF, BLK),
         vm(2, HALF, BLK), vm(HALF, BLK), vm(HALF, BLK),
-        vm(LANES, 2, 16, BLK), vm(15, 16, BLK), vm(2, 16, 256), vm(16, 256), vf(8, 2, 8, 128),
+        vf(LANES, 8, BLK), vm(LANES, 2, 16, BLK), vm(15, 16, BLK), vm(2, 16, 256), vm(16, 256), vf(8, 2, 8, 128),
         vf(7, 2, 8, 128), vf(18, 8, 128), vm(2, 8, 9, 16, 128),
         dma(21), dma(30), dma(30), dma(2, 2, 6), dma(2, 2, 6), dma(3, 2), dma(3, 2),
-        dma(3), dma(3), dma(12), dma(12), dma(2, 6), dma(2, 6), dma(5, 16), dma(5, 16),
+        dma(3), dma(3), dma(15), dma(15), dma(2, 6), dma(2, 6), dma(5, 16), dma(5, 16),
     ]
     dx, dgrad, small = pl.pallas_call(
         kernel,
@@ -766,7 +796,7 @@
         ),
     )(
         normed, output_gradient, wq, kvt, output_weight, adapter_down.reshape(3 * RANK, width),
-        query_up, key_value_up.reshape(RANK, 64), output_down, output_up, cos_wide, sin_wide,
+        query_up, key_value_up, output_down, output_up, cos, sin,
     )
     return tuple(
         pl.pallas_call(

time: 150 us -> 147 us (0.980); the launches traced: 148 us -> 146 us
    sin x0 -> x1, other arithmetic: none -> 1.8 us  [body(): cos, sin = (jnp.cos(angles), jnp.sin(angles))]
where the time goes in v4:
time: 147 us; the launch traced here: 146 us
  Pallas kernels  144 us (98%)
  other arithmetic  1.83 us (1%)
    pallas_call x1, Pallas kernels, body(): pl.pallas_call(kernel, out_shape=out_shape, in_specs=[hbm] * 5 + [vmem] *...  142 us

profile of v4, /device:TPU:48, one launch (start us, length us, event | category | flops | bytes accessed | tf_op | source)
XLA Modules:
  0.0 146.5 jit_solution(12424402679916154969)
XLA Ops:
  0.7 1.8 %multiply_sine_fusion = (f32[2,256,64]{2,1,0:T(8,128)}, f32[2,256,64]{2,1,0:T(8,128)}) fusion(f32[64]{0:T(128)S(1)} %multiply_power_fusion, f32[2,256]{1,0:T(2,128)S(1)} %fusion.1), kind=kLoop, calls=%fused_computation | loop fusion | flops 32768 | bytes 264448 | tf_op jit(solution)/shard_map/sin | solution.py:745
  2.5 141.6 %shard_map.145 = (bf16[512,512]{1,0:T(8,128)(2,1)}, f32[24,8192]{1,0:T(8,128)}, f32[24,512]{1,0:T(8,128)}) custom-call(bf16[512,512]{1,0:T(8,128)(2,1)} %x_ref.1, bf16[512,512]{1,0:T(8,128)(2,1)} %g_ref.1, bf16[8,2,512,256]{3,2,1,0:T(8,128)(2,1)} %bitcast.3, bf16[2,32,8192]{2,1,0:T(8,128)(2,1)} %bitcast.4, bf16[256,8192]{1,0:T(8,128)(2,1)} %wo_ref.1, ...), custom_call_target="tpu_custom_call" | custom-call | flops 8999999488 | bytes 20000000 | tf_op jit(solution)/shard_map/pallas_call | solution.py:785
  144.1 2.4 %shard_map.146 = (bf16[512,512]{1,0:T(8,128)(2,1)}, f32[3,8,8192]{2,1,0:T(8,128)}, f32[8,256]{1,0:T(8,128)}, f32[8,2,32]{2,1,0:T(2,128)}, f32[8,256]{1,0:T(8,128)}, /*index=5*/f32[8,512]{1,0:T(8,128)}) custom-call(bf16[512,512]{1,0:T(8,128)(2,1)} %get-tuple-element.9.dx_ref, f32[24,8192]{1,0:T(8,128)} %get-tuple-element.10.dgrad_ref, ...), custom_call_target="tpu_custom_call" | custom-call | tf_op jit(solution)/shard_map/pallas_call | solution.py:802
  (2 shorter events, 0.0 us)

commit v5 on v4

--- a/solution.py
+++ b/solution.py
@@ -623,11 +623,9 @@
         total = dx_block(lane_of(1, 0), i)
         arrived(rsr.at[1, slot], rs_recv.at[1, slot])
         yst[i] = (total + rsr[1, slot].astype(F32)).astype(BF16)
-        half = i + p - 2 * i * p
-        push(yst.at[i], yrecv.at[half], y_send.at[2, i], y_recv.at[2, half],
-             dev(lax.rem(s + i * p, SEQ), across))
-    side_home(1, 0, 0)
+        push(yst.at[i], yrecv.at[1 - i], y_send.at[2, i], y_recv.at[2, 1 - i], beyond[i])
     side_home(-1, 1, 1)
+    side_home(1, 1, None)
     for d in range(1, 16):
         m = lax.rem(place_in_plane - d + 16, 16)
         arrived(tiles.at[m], s_recv.at[2, d])
@@ -637,7 +635,7 @@
     for d in range(1, 8):
         push(eb.at[c, z], eb.at[c, z], s_send.at[3, d], s_recv.at[3, d],
              dev(column_peer(d) * 2 + k_lo, h))
-    side_home(1, 1, None)
+    side_home(1, 0, 0)
     side_home(-1, 0, None)
     after = lax.rem(s + 1, SEQ)
 
@@ -650,7 +648,8 @@
         for k in (2, 4):
             arrived(rsr.at[0, k + i], rs_recv.at[0, k + i])
             total += rsr[0, k + i].astype(F32)
-        rown[i] = total
+        arrived(yrecv.at[i], y_recv.at[2, i])
+        rown[i] = total + yrecv[i].astype(F32)
         if i == 1:
 
             @pl.when(p == 1)
@@ -679,19 +678,16 @@
         axis=1,
     )
 
-    for half in range(2):
-        arrived(yrecv.at[half], y_recv.at[2, half])
-
     @pl.when(p == 0)
     def _():
         for i in range(2):
-            dx_ref[i * HALF : i * HALF + HALF, :] = (rown[i] + yrecv[i].astype(F32)).astype(BF16)
+            dx_ref[i * HALF : i * HALF + HALF, :] = rown[i].astype(BF16)
 
     @pl.when(p == 1)
     def _():
+        dx_ref[HALF:ROWS, :] = rown[0].astype(BF16)
         arrived(rollrecv, roll_recv.at[2])
-        dx_ref[HALF:ROWS, :] = (rown[0] + yrecv[1].astype(F32)).astype(BF16)
-        dx_ref[0:HALF, :] = (rollrecv[...].astype(F32) + yrecv[0].astype(F32)).astype(BF16)
+        dx_ref[0:HALF, :] = rollrecv[...]
 
     arrived(eb.at[1 - c], s_recv.at[4, 0])
 

time: 147 us -> 143 us (0.973)
  Pallas kernels: 144 us -> 139 us
    pallas_call x1, Pallas kernels: 142 us -> 137 us  [body(): pl.pallas_call(kernel, out_shape=out_shape, in_specs=[hbm] * 5 + [vmem] *...]
where the time goes in v5:
time: 143 us; the launch traced here: 142 us
  Pallas kernels  139 us (97%)
  other arithmetic  1.83 us (1%)
    pallas_call x1, Pallas kernels, body(): pl.pallas_call(kernel, out_shape=out_shape, in_specs=[hbm] * 5 + [vmem] *...  137 us

profile of v5, /device:TPU:48, one launch (start us, length us, event | category | flops | bytes accessed | tf_op | source)
XLA Modules:
  0.0 142.0 jit_solution(619797932034504937)
XLA Ops:
  0.7 1.8 %multiply_sine_fusion = (f32[2,256,64]{2,1,0:T(8,128)}, f32[2,256,64]{2,1,0:T(8,128)}) fusion(f32[64]{0:T(128)S(1)} %multiply_power_fusion, f32[2,256]{1,0:T(2,128)S(1)} %fusion.1), kind=kLoop, calls=%fused_computation | loop fusion | flops 32768 | bytes 264448 | tf_op jit(solution)/shard_map/sin | solution.py:741
  2.5 137.1 %shard_map.145 = (bf16[512,512]{1,0:T(8,128)(2,1)}, f32[24,8192]{1,0:T(8,128)}, f32[24,512]{1,0:T(8,128)}) custom-call(bf16[512,512]{1,0:T(8,128)(2,1)} %x_ref.1, bf16[512,512]{1,0:T(8,128)(2,1)} %g_ref.1, bf16[8,2,512,256]{3,2,1,0:T(8,128)(2,1)} %bitcast.3, bf16[2,32,8192]{2,1,0:T(8,128)(2,1)} %bitcast.4, bf16[256,8192]{1,0:T(8,128)(2,1)} %wo_ref.1, ...), custom_call_target="tpu_custom_call" | custom-call | flops 8999999488 | bytes 20000000 | tf_op jit(solution)/shard_map/pallas_call | solution.py:781
  139.6 2.4 %shard_map.146 = (bf16[512,512]{1,0:T(8,128)(2,1)}, f32[3,8,8192]{2,1,0:T(8,128)}, f32[8,256]{1,0:T(8,128)}, f32[8,2,32]{2,1,0:T(2,128)}, f32[8,256]{1,0:T(8,128)}, /*index=5*/f32[8,512]{1,0:T(8,128)}) custom-call(bf16[512,512]{1,0:T(8,128)(2,1)} %get-tuple-element.9.dx_ref, f32[24,8192]{1,0:T(8,128)} %get-tuple-element.10.dgrad_ref, ...), custom_call_target="tpu_custom_call" | custom-call | tf_op jit(solution)/shard_map/pallas_call | solution.py:798
  (2 shorter events, 0.0 us)

commit v6 on v5

--- a/solution.py
+++ b/solution.py
@@ -467,7 +467,7 @@
         ups[j] = total[0:8]
         return carry
 
-    lax.fori_loop(0, LANES, out_up, 0)
+    lax.fori_loop(0, LANES // 2, out_up, 0)
 
     kv_rows = kvf[0:32, :].astype(F32)
     kv_low = jnp.concatenate([kv_rows[:, 0:64], kv_rows[:, 128:192]], axis=1)
@@ -477,6 +477,7 @@
     sib_up = jnp.concatenate([qups[...], jnp.zeros((112, 256), BF16)], axis=0)
 
     pass_on(0)
+    lax.fori_loop(LANES // 2, LANES, out_up, 0)
     arrived(dq1, m_recv.at[8])
     for kind in (1, 0):
         arrived(dkvr.at[2, kind], m_recv.at[10 + 3 * kind])

time: 143 us -> 142 us (level)
  no operation moved by 1% of the time
where the time goes in v6:
time: 142 us
  Pallas kernels  139 us (98%)
  other arithmetic  1.83 us (1%)
    pallas_call x1, Pallas kernels, body(): pl.pallas_call(kernel, out_shape=out_shape, in_specs=[hbm] * 5 + [vmem] *...  137 us

profile of v6, /device:TPU:48, one launch (start us, length us, event | category | flops | bytes accessed | tf_op | source)
XLA Modules:
  0.0 141.8 jit_solution(10677972369816220235)
XLA Ops:
  0.7 1.8 %multiply_sine_fusion = (f32[2,256,64]{2,1,0:T(8,128)}, f32[2,256,64]{2,1,0:T(8,128)}) fusion(f32[64]{0:T(128)S(1)} %multiply_power_fusion, f32[2,256]{1,0:T(2,128)S(1)} %fusion.1), kind=kLoop, calls=%fused_computation | loop fusion | flops 32768 | bytes 264448 | tf_op jit(solution)/shard_map/sin | solution.py:742
  2.5 136.9 %shard_map.145 = (bf16[512,512]{1,0:T(8,128)(2,1)}, f32[24,8192]{1,0:T(8,128)}, f32[24,512]{1,0:T(8,128)}) custom-call(bf16[512,512]{1,0:T(8,128)(2,1)} %x_ref.1, bf16[512,512]{1,0:T(8,128)(2,1)} %g_ref.1, bf16[8,2,512,256]{3,2,1,0:T(8,128)(2,1)} %bitcast.3, bf16[2,32,8192]{2,1,0:T(8,128)(2,1)} %bitcast.4, bf16[256,8192]{1,0:T(8,128)(2,1)} %wo_ref.1, ...), custom_call_target="tpu_custom_call" | custom-call | flops 8999999488 | bytes 20000000 | tf_op jit(solution)/shard_map/pallas_call | solution.py:782
  139.4 2.4 %shard_map.146 = (bf16[512,512]{1,0:T(8,128)(2,1)}, f32[3,8,8192]{2,1,0:T(8,128)}, f32[8,256]{1,0:T(8,128)}, f32[8,2,32]{2,1,0:T(2,128)}, f32[8,256]{1,0:T(8,128)}, /*index=5*/f32[8,512]{1,0:T(8,128)}) custom-call(bf16[512,512]{1,0:T(8,128)(2,1)} %get-tuple-element.9.dx_ref, f32[24,8192]{1,0:T(8,128)} %get-tuple-element.10.dgrad_ref, ...), custom_call_target="tpu_custom_call" | custom-call | tf_op jit(solution)/shard_map/pallas_call | solution.py:799
  (2 shorter events, 0.0 us)
